TPU v7x, 32 devices: a whole 2x2x4 slice. The times are simulated.
32 devices in a mesh: groups: 2 (over x), row: 16 (over z, y, core).
Axes of the slice: x: 2, y: 2, z: 4, core: 2. Of those that a mesh axis runs over, the one named last changes fastest.
Arguments:
- pair_rows: bfloat16 [256, 128, 128], P(('groups', 'row')), parts along dimension 0, may hold values from -6 to 6
- in_gain: float32 [128], replicated, may hold values from 0.1 to 1.9
- w_left: bfloat16 [128, 128], replicated, may hold values from -0.5 to 0.5
- w_left_gate: bfloat16 [128, 128], replicated, may hold values from -0.5 to 0.5
- w_right: bfloat16 [128, 128], replicated, may hold values from -0.5 to 0.5
- w_right_gate: bfloat16 [128, 128], replicated, may hold values from -0.5 to 0.5
- w_gate: bfloat16 [128, 128], replicated, may hold values from -0.5 to 0.5
- w_out: bfloat16 [128, 128], replicated, may hold values from -0.5 to 0.5
- out_gain: float32 [128], replicated, may hold values from 0.1 to 1.9
- valid_len: int32 [2], P('groups'), parts along dimension 0, may hold values from 64 to 128
- window: int32 [2], P('groups'), parts along dimension 0, may hold values from 0 to 7
Outputs:
- update: bfloat16 [256, 16, 128], P(('groups', 'row')), parts along dimension 0
There are 2 independent parts, one for each index of `groups`. A program takes and returns all parts, laid end to end along the dimension named above; an argument that names none is the same for every part. Nothing has to cross between parts.
All inputs are finite; a program needn't handle non-finite values.
Results may differ from a plain program's by a relative error of at most 0.0078.
Values may be sent and summed in bfloat16 or wider, within the bound.
No kernel may reach another device: no remote copies, remote signals or barrier semaphores. Data moves between devices by JAX's collectives and lax.ppermute only.
A program may use at most 128 MiB of HBM per device.

v0:
```python
import jax
import jax.numpy as jnp
from jax import lax
from jax.sharding import PartitionSpec as P


def layer_norm(values, gain):
    mean_v = jnp.mean(values, axis=-1, keepdims=True)
    centered = values - mean_v
    variance_v = jnp.mean(centered * centered, axis=-1, keepdims=True)
    return centered * lax.rsqrt(variance_v + 1e-05) * gain


def on_device(
    pair_rows,
    in_gain,
    w_left,
    w_left_gate,
    w_right,
    w_right_gate,
    w_gate,
    w_out,
    out_gain,
    valid_len,
    window,
):
    my_index = lax.axis_index("row")
    local_rows, tokens_all, channels = pair_rows.shape
    width_win = tokens_all // 8
    valid_upto = valid_len[0]
    start_block = window[0]
    start_row = start_block * width_win
    row_ids = my_index * local_rows + jnp.arange(local_rows, dtype=jnp.int32)
    row_live = (row_ids < valid_upto).astype(jnp.float32)
    col_live = (jnp.arange(tokens_all, dtype=jnp.int32) < valid_upto).astype(jnp.float32)
    live_mask = (row_live[:, None] * col_live[None, :])[:, :, None]
    normed = layer_norm(pair_rows.astype(jnp.float32), in_gain).astype(jnp.bfloat16)
    flat_rows = normed.reshape(-1, channels)
    joined = jnp.concatenate([w_left, w_left_gate, w_right, w_right_gate], axis=1)
    projected = jnp.dot(flat_rows, joined, preferred_element_type=jnp.float32)
    projected = projected.reshape(local_rows, tokens_all, 4 * channels)
    left_edge = (
        jax.nn.sigmoid(projected[:, :, channels : 2 * channels])
        * projected[:, :, :channels]
        * live_mask
    ).astype(jnp.bfloat16)
    right_edge = (
        jax.nn.sigmoid(projected[:, :, 3 * channels :])
        * projected[:, :, 2 * channels : 3 * channels]
        * live_mask
    ).astype(jnp.bfloat16)
    gate_in = lax.dynamic_slice_in_dim(normed, start_row, width_win, 1)
    gate_vals = jax.nn.sigmoid(
        jnp.dot(gate_in.reshape(-1, channels), w_gate, preferred_element_type=jnp.float32)
    )
    gate_vals = gate_vals.reshape(local_rows, width_win, channels)
    regrouped = lax.all_to_all(right_edge, "row", split_axis=1, concat_axis=0, tiled=True)
    picked = lax.dynamic_slice_in_dim(regrouped, start_row, width_win, 0)
    window_right = lax.all_gather(picked, "row", axis=1, tiled=True)
    product = jnp.einsum(
        "ikc,jkc->ijc", left_edge, window_right, preferred_element_type=jnp.float32
    )
    normed_out = layer_norm(product, out_gain).astype(jnp.bfloat16)
    result = jnp.dot(normed_out.reshape(-1, channels), w_out, preferred_element_type=jnp.float32)
    return (gate_vals * result.reshape(local_rows, width_win, channels)).astype(jnp.bfloat16)


def solution(mesh):
    return jax.shard_map(
        on_device,
        mesh=mesh,
        in_specs=(
            P(("groups", "row"), None, None),
            P(),
            P(),
            P(),
            P(),
            P(),
            P(),
            P(),
            P(),
            P("groups"),
            P("groups"),
        ),
        out_specs=P(("groups", "row"), None, None),
        check_vma=False,
    )
```

profile of v0, /device:TPU:31, one launch (start us, length us, event | category | flops | bytes accessed | tf_op | source)
XLA Modules:
  0.0 78.5 jit_solution(6741622553419118071)
XLA Ops:
  0.0 0.0 copy-start
  0.7 1.1 %convert_reduce_fusion = f32[8,128]{1,0:T(8,128)S(1)} fusion(bf16[8,128,128]{2,1,0:T(8,128)(2,1)} %param.11), kind=kLoop, calls=%fused_computation.7 | loop fusion | flops 261120 | bytes 266240 | tf_op jit(solution)/shard_map/reduce_sum | solution.py:8
  1.8 1.3 %fusion.6 = f32[8,128]{1,0:T(8,128)S(1)} fusion(bf16[8,128,128]{2,1,0:T(8,128)(2,1)} %param.11, f32[8,128]{1,0:T(8,128)S(1)} %broadcast_multiply_fusion.2), kind=kLoop, calls=%fused_computation.10 | loop fusion | flops 523264 | bytes 270336 | tf_op jit(solution)/shard_map/reduce_sum | solution.py:10
  3.1 0.1 broadcast_multiply_fusion.1
  3.2 1.3 %fusion.8 = bf16[8,128,128]{2,1,0:T(8,128)(2,1)S(1)} fusion(bf16[8,128,128]{2,1,0:T(8,128)(2,1)} %param.11, f32[128]{0:T(128)} %param.12, f32[8,128]{1,0:T(8,128)S(1)} %add_rsqrt_fusion.1, f32[8,128]{1,0:T(8,128)S(1)} %broadcast_multiply_fusion.2), kind=kLoop, calls=%fused_computation.12 | loop fusion | flops 655360 | bytes 532992 | tf_op jit(solution)/shard_map/convert_element_type | solution.py:37
  4.5 1.2 %fusion.19 = f32[8,128,512]{2,1,0:T(8,128)S(1)} fusion(bf16[8,128,128]{2,1,0:T(8,128)(2,1)S(1)} %fusion.8, bf16[128,128]{1,0:T(8,128)(2,1)} %param.16, bf16[128,128]{1,0:T(8,128)(2,1)} %param.15, bf16[128,128]{1,0:T(8,128)(2,1)} %param.14, bf16[128,128]{1,0:T(8,128)(2,1)} %param.13), kind=kOutput, calls=%fused_computation.28 | convolution fusion | flops 134742016 | bytes 2490368 | tf_op jit(solution)/shard_map/dot_general | solution.py:40
  5.7 0.3 fusion.10
  6.0 0.9 %copy.29 = bf16[8,128,128]{2,0,1:T(8,128)(2,1)} copy(bf16[8,128,128]{2,1,0:T(8,128)(2,1)S(1)} %get-tuple-element.6) | data formatting | bytes 524288 | tf_op jit(solution)/shard_map/convert_element_type | solution.py:51
  6.9 6.3 %all-to-all-start = ((bf16[8,128,128]{2,0,1:T(8,128)(2,1)}), bf16[8,128,128]{2,0,1:T(8,128)(2,1)S(1)}, u32[]{:S(2)}, u32[]{:S(2)}) async-start(bf16[8,128,128]{2,0,1:T(8,128)(2,1)} %copy.29), calls=%async_computation | async-start | bytes 524288 | tf_op jit(solution)/shard_map/all_to_all | solution.py:57
  13.9 0.2 copy.33
  14.1 0.0 copy-done
  14.1 0.2 fusion.2
  14.3 6.0 %all-to-all-done = bf16[8,128,128]{2,0,1:T(8,128)(2,1)S(1)} async-done(((bf16[8,128,128]{2,0,1:T(8,128)(2,1)}), bf16[8,128,128]{2,0,1:T(8,128)(2,1)S(1)}, u32[]{:S(2)}, u32[]{:S(2)}) %all-to-all-start) | async-done | bytes 262176 | tf_op jit(solution)/shard_map/all_to_all | solution.py:57
  20.4 0.2 copy.36
  20.6 0.0 copy-start.1
  20.6 0.0 copy-start.2
  20.6 55.3 %all_gather.3 = bf16[16,128,128]{0,1,2:T(8,128)(2,1)S(1)} all-gather(bf16[16,8,128]{0,1,2:T(8,128)(2,1)S(1)} %copy.36), channel_id=1, replica_groups=mesh['groups'=2,'row'=16] {'row'}, dimensions={1}, use_global_device_ids=true | all-gather | bytes 557056 | tf_op jit(solution)/shard_map/all_gather | solution.py:59
  75.9 1.2 %fusion.31 = f32[128,16,8]{1,2,0:T(8,128)S(1)} fusion(bf16[16,128,128]{0,1,2:T(8,128)(2,1)S(1)} %all_gather.3, bf16[8,128,128]{1,0,2:T(8,128)(2,1)S(1)} %copy.33), kind=kOutput, calls=%fused_computation.53 | convolution fusion | flops 4194304 | bytes 851968 | tf_op jit(solution)/shard_map/ikc,jkc->ijc/dot_general | solution.py:60
  77.1 0.2 copy.34
  77.3 0.1 bitcast_reduce_fusion
  77.4 0.2 multiply_reduce_fusion
  77.6 0.0 copy-done.1
  77.6 0.0 copy-done.2
  77.6 0.8 %fusion.3 = bf16[8,16,128]{2,1,0:T(8,128)(2,1)} fusion(f32[8,16,128]{2,1,0:T(8,128)S(1)} %bitcast.31, f32[128,16,8]{0,1,2:T(8,128)S(1)} %copy.34, bf16[128,128]{1,0:T(8,128)(2,1)S(1)} %copy-done.1, f32[128]{0:T(128)S(1)} %copy-done.2, f32[8,16]{1,0:T(8,128)S(1)} %add_rsqrt_fusion, f32[8,16]{1,0:T(8,128)S(1)} %broadcast_multiply_fusion), kind=kOutput, calls=%fused_computation.5 | convolution fusion | flops 4292608 | bytes 198144 | tf_op jit(solution)/shard_map/dot_general | solution.py:64
  (9 shorter events, 0.1 us)
Async XLA Ops:
  0.0 14.1 %copy-start = (bf16[128,128]{1,0:T(8,128)(2,1)S(1)}, bf16[128,128]{1,0:T(8,128)(2,1)}, u32[]{:S(2)}) copy-start(bf16[128,128]{1,0:T(8,128)(2,1)} %param.17) | copy-start | bytes 98308
  6.9 13.4 %all-to-all-start = ((bf16[8,128,128]{2,0,1:T(8,128)(2,1)}), bf16[8,128,128]{2,0,1:T(8,128)(2,1)S(1)}, u32[]{:S(2)}, u32[]{:S(2)}) async-start(bf16[8,128,128]{2,0,1:T(8,128)(2,1)} %copy.29), calls=%async_computation | async-start | bytes 524288 | tf_op jit(solution)/shard_map/all_to_all | solution.py:57
  20.6 57.0 %copy-start.1 = (bf16[128,128]{1,0:T(8,128)(2,1)S(1)}, bf16[128,128]{1,0:T(8,128)(2,1)}, u32[]{:S(2)}) copy-start(bf16[128,128]{1,0:T(8,128)(2,1)} %param.18) | copy-start | bytes 98308
  20.6 57.0 %copy-start.2 = (f32[128]{0:T(128)S(1)}, f32[128]{0:T(128)}, u32[]{:S(2)}) copy-start(f32[128]{0:T(128)} %param.19) | copy-start | bytes 1540
where the time goes:
time: 78.9 us; the launch traced here: 78.5 us
  blocking collectives  55.3 us (70%)
  starting transfers between devices  6.34 us (8%)
  waiting for transfers between devices  6 us (8%)
  other arithmetic  4.38 us (6%)
  matrix products  3.4 us (4%)
  local copies, waits for them, and re-layouts  1.53 us (2%)
  between operations  1.5 us (2%)
    all_gather x1, blocking collectives, on_device(): window_right = lax.all_gather(picked, 'row', axis=1, tiled=True)  55.3 us
    all_to_all x1, starting transfers between devices, on_device(): lax.all_to_all(right_edge, 'row', split_axis=1, concat_axis=0, tiled=True)  6.34 us
    all_to_all x1, waiting for transfers between devices, on_device(): lax.all_to_all(right_edge, 'row', split_axis=1, concat_axis=0, tiled=True)  6 us
  transfers between devices with their start and end apart: 1, of which 1 were waited for; matrix products, arithmetic and copies ran while one was open for 0% of the time, Pallas kernels for 0%

commit v1 on v0

v1 whole, which is shorter than its diff:
```python
import functools

import jax
import jax.numpy as jnp
from jax import lax
from jax.experimental import pallas as pl
from jax.experimental.pallas import tpu as pltpu
from jax.sharding import PartitionSpec as P

BLOCKS = 8
VMEM = pl.BlockSpec(memory_space=pltpu.VMEM)
SMEM = pl.BlockSpec(memory_space=pltpu.SMEM)


def sigmoid(values):
    return 0.5 * jnp.tanh(0.5 * values) + 0.5


def layer_norm(values, gain):
    scale = 1.0 / values.shape[-1]
    mean_v = jnp.sum(values, axis=-1, keepdims=True) * scale
    centered = values - mean_v
    variance_v = jnp.sum(centered * centered, axis=-1, keepdims=True) * scale
    return centered * lax.rsqrt(variance_v + 1e-05) * gain


def dot(left, right):
    return jnp.dot(left, right, preferred_element_type=jnp.float32)


def edge_chunk(x, gain, w, w_gating, live):
    normed = layer_norm(x.astype(jnp.float32), gain).astype(jnp.bfloat16)
    value = dot(normed, w)
    gating = dot(normed, w_gating)
    return normed, (sigmoid(gating) * value * live).astype(jnp.bfloat16)


def steps(count, body):
    if count <= 16:
        for step in range(count):
            body(step)
    else:
        pl.loop(0, count)(body)


def edge_body(chunk, scalars, x_ref, gain_ref, w_ref, wg_ref, out_ref):
    rows, tokens, _ = x_ref.shape
    per_row = tokens // chunk
    gain = gain_ref[...]
    valid, first = scalars[0], scalars[1]
    ids = lax.broadcasted_iota(jnp.int32, (chunk, 1), 0)

    def body(step):
        row, col = step // per_row, (step % per_row) * chunk
        here = jnp.logical_and(first + row < valid, ids + col < valid)
        _, edge = edge_chunk(
            x_ref[row, pl.ds(col, chunk), :], gain, w_ref[...], wg_ref[...], here.astype(jnp.float32)
        )
        out_ref[row, pl.ds(col, chunk), :] = edge.astype(out_ref.dtype)

    steps(rows * per_row, body)


def left_body(chunk, scalars, x_ref, gain_ref, w_ref, wg_ref, wo_ref, out_ref, gate_ref):
    edge_body(chunk, scalars, x_ref, gain_ref, w_ref, wg_ref, out_ref)
    rows, width, channels = gate_ref.shape
    start = pl.multiple_of(scalars[2], width)
    gain = gain_ref[...]

    def body(row):
        x = x_ref[row, pl.ds(start, width), :]
        normed = layer_norm(x.astype(jnp.float32), gain).astype(jnp.bfloat16)
        gate_ref[row] = sigmoid(dot(normed, wo_ref[...]))

    steps(rows, body)


def finish_body(pieces, left_ref, gate_ref, w_out_ref, gain_ref, *refs):
    right_refs, out_ref, product = refs[:pieces], refs[-2], refs[-1]
    rows, tokens, channels = left_ref.shape
    base = 0
    for right_ref in right_refs:
        height = right_ref.shape[0]

        def body(j, right_ref=right_ref, base=base):
            def over(k, acc):
                at = pl.ds(k * 128, 128)
                r = right_ref[j, at, :].astype(jnp.float32).reshape(-1, 8, channels)
                return tuple(
                    acc[i]
                    + jnp.sum(left_ref[i, at, :].astype(jnp.float32).reshape(-1, 8, channels) * r, axis=0)
                    for i in range(rows)
                )

            acc = tuple(jnp.zeros((8, channels), jnp.float32) for _ in range(rows))
            if tokens == 128:
                acc = over(0, acc)
            else:
                acc = lax.fori_loop(0, tokens // 128, over, acc)
            for i in range(rows):
                product[i, pl.ds(base + j, 1), :] = jnp.sum(acc[i], axis=0, keepdims=True)

        steps(height, body)
        base += height
    gain = gain_ref[...]
    flat = product[...].reshape(rows * base, channels)
    normed = layer_norm(flat, gain).astype(jnp.bfloat16)
    result = dot(normed, w_out_ref[...]).reshape(rows, base, channels)
    out_ref[...] = (gate_ref[...] * result).astype(jnp.bfloat16)


def local(body, out_shape, n_in, scratch=(), smem=True):
    return pl.pallas_call(
        body,
        out_shape=out_shape,
        in_specs=([SMEM] if smem else []) + [VMEM] * (n_in - int(smem)),
        out_specs=jax.tree.map(lambda _: VMEM, out_shape),
        scratch_shapes=list(scratch),
        compiler_params=pltpu.CompilerParams(vmem_limit_bytes=60 * 2**20),
    )


def on_device(
    pair_rows, in_gain, w_left, w_left_gate, w_right, w_right_gate, w_gate, w_out, out_gain, valid_len, window, devices
):
    rows, tokens, channels = pair_rows.shape
    width = tokens // BLOCKS
    parts = width // rows
    half = rows // 2
    chunk = min(tokens, 128)
    me = lax.axis_index("row").astype(jnp.int32)
    block, part = me // parts, me % parts
    sub = block % 2
    valid, start = valid_len[0], window[0] * width
    differs = block ^ window[0]
    in_gain = in_gain.reshape(1, channels)
    out_gain = out_gain.reshape(1, channels)
    bf16, f32 = jnp.bfloat16, jnp.float32

    def swap(values, mask):
        return lax.ppermute(values, "row", [(i, i ^ mask) for i in range(devices)])

    halves = pair_rows.reshape(2, half, tokens, channels)
    sent = lax.dynamic_index_in_dim(halves, 1 - sub, 0, keepdims=False)
    kept = lax.dynamic_index_in_dim(halves, sub, 0, keepdims=False)
    piece = jnp.where(differs & 1 == 0, kept, swap(sent, parts))

    left, gate = local(
        functools.partial(left_body, chunk),
        (
            jax.ShapeDtypeStruct((rows, tokens, channels), bf16),
            jax.ShapeDtypeStruct((rows, width, channels), f32),
        ),
        6,
    )(jnp.stack([valid, me * rows, start]), pair_rows, in_gain, w_left, w_left_gate, w_gate)

    bit = 2
    while bit < BLOCKS:
        piece = jnp.where(differs & bit == 0, piece, swap(piece, parts * bit))
        bit *= 2

    first = start + part * rows + sub * half
    right = local(
        functools.partial(edge_body, chunk), jax.ShapeDtypeStruct((half, tokens, channels), bf16), 5
    )(jnp.stack([valid, first, start]), piece, in_gain, w_right, w_right_gate)

    held = [right, swap(right, parts)]
    order = [(0, 0), (0, 1)]
    bit = 1
    while bit < parts:
        held = held + [swap(values, bit) for values in held]
        order = order + [(p ^ bit, s) for p, s in order]
        bit *= 2

    def to_slots(values):
        values = jnp.where(sub == 0, values, values[:, :, ::-1])
        bit = 1
        while bit < parts:
            view = values.reshape(rows, parts // (2 * bit), 2, bit, 2, half, channels)
            values = jnp.where(part & bit == 0, view, view[:, :, ::-1]).reshape(values.shape)
            bit *= 2
        return values

    gate_slots = to_slots(gate.reshape(rows, parts, 2, half, channels)).reshape(rows, width, channels)
    out = local(
        functools.partial(finish_body, len(held)),
        jax.ShapeDtypeStruct((rows, width, channels), bf16),
        4 + len(held),
        [pltpu.VMEM((rows, width, channels), f32)],
        smem=False,
    )(left, gate_slots, w_out, out_gain, *held)
    return to_slots(out.reshape(rows, parts, 2, half, channels)).reshape(rows, width, channels)


def solution(mesh):
    return jax.shard_map(
        functools.partial(on_device, devices=mesh.shape["row"]),
        mesh=mesh,
        in_specs=(P(("groups", "row"), None, None),) + (P(),) * 8 + (P("groups"),) * 2,
        out_specs=P(("groups", "row"), None, None),
        check_vma=False,
    )
```

time: 78.9 us -> 34.5 us (0.44)
  the two profiles are of different devices: /device:TPU:31 before, /device:TPU:0 now
where the time goes in v1:
time: 34.5 us; the launch traced here: 34.2 us
  waiting for transfers between devices  10.3 us (30%)
  starting transfers between devices  9.58 us (28%)
  Pallas kernels  7.19 us (21%)
  other arithmetic  4.04 us (12%)
  local copies, waits for them, and re-layouts  1.65 us (5%)
  between operations  1.37 us (4%)
    ppermute x6, waiting for transfers between devices, swap(): return lax.ppermute(values, 'row', [(i, i ^ mask) for i in range(devices)])  10.3 us
    ppermute x6, starting transfers between devices, swap(): return lax.ppermute(values, 'row', [(i, i ^ mask) for i in range(devices)])  9.58 us
    pallas_call x1, Pallas kernels, on_device(): local(functools.partial(finish_body, len(held)), jax.ShapeDtypeStruct((ro...  2.86 us
    pallas_call x1, Pallas kernels, on_device(): local(functools.partial(left_body, chunk), (jax.ShapeDtypeStruct((rows, t...  2.29 us
    pallas_call x1, Pallas kernels, on_device(): local(functools.partial(edge_body, chunk), jax.ShapeDtypeStruct((half, to...  2.05 us
    select_n x2, other arithmetic, to_slots(): jnp.where(part & bit == 0, view, view[:, :, ::-1]).reshape(values.shape)  1.31 us
    squeeze x1, local copies, waits for them, and re-layouts, on_device(): sent = lax.dynamic_index_in_dim(halves, 1 - sub, 0, keepdims=False)  0.99 us
    select_n x2, other arithmetic, to_slots(): values = jnp.where(sub == 0, values, values[:, :, ::-1])  0.87 us
  transfers between devices with their start and end apart: 6, of which 5 were waited for; matrix products, arithmetic and copies ran while one was open for 5% of the time, Pallas kernels for 7%

profile of v1, /device:TPU:0, one launch (start us, length us, event | category | flops | bytes accessed | tf_op | source)
XLA Modules:
  0.0 34.2 jit_solution(15209254849929527027)
XLA Ops:
  0.0 0.0 copy-start
  0.0 1.0 %dynamic-slice_bitcast_fusion = bf16[4,128,128]{2,1,0:T(8,128)(2,1)S(1)} fusion(bf16[2,4,128,128]{3,2,1,0:T(8,128)(2,1)} %bitcast.17, s32[]{:T(128)S(6)} %select_n.83), kind=kLoop, calls=%fused_computation.1 | loop fusion | bytes 262148 | tf_op jit(solution)/shard_map/jit(dynamic_index_in_dim)/squeeze | solution.py:144
  1.0 3.0 %collective-permute-start = (bf16[4,128,128]{2,1,0:T(8,128)(2,1)S(1)}, bf16[4,128,128]{2,1,0:T(8,128)(2,1)S(1)}, u32[]{:S(2)}, u32[]{:S(2)}) collective-permute-start(bf16[4,128,128]{2,1,0:T(8,128)(2,1)S(1)} %dynamic-slice_bitcast_fusion), channel_id=1, source_target_pairs={{0,2},{1,3},{2,0},{3,1},{4,6},{5,7},{6,4},{7,5},{8,10},{9,11},{10,... | collective-permute-start | bytes 393224 | tf_op jit(solution)/shard_map/ppermute | solution.py:141
  4.7 2.8 %collective-permute-done = bf16[4,128,128]{2,1,0:T(8,128)(2,1)S(1)} collective-permute-done((bf16[4,128,128]{2,1,0:T(8,128)(2,1)S(1)}, bf16[4,128,128]{2,1,0:T(8,128)(2,1)S(1)}, u32[]{:S(2)}, u32[]{:S(2)}) %collective-permute-start) | collective-permute-done | bytes 131104 | tf_op jit(solution)/shard_map/ppermute | solution.py:141
  7.5 0.0 copy-done
  7.5 1.9 %collective-permute-start.1 = (bf16[4,128,128]{2,1,0:T(8,128)(2,1)S(1)}, bf16[4,128,128]{2,1,0:T(8,128)(2,1)S(1)}, u32[]{:S(2)}, u32[]{:S(2)}) collective-permute-start(bf16[4,128,128]{2,1,0:T(8,128)(2,1)S(1)} %bitcast_select_fusion), channel_id=1, source_target_pairs={{0,4},{1,5},{2,6},{3,7},{4,0},{5,1},{6,2},{7,3},{8,12},{9,13},{10,... | collective-permute-start | bytes 393224 | tf_op jit(solution)/shard_map/ppermute | solution.py:141
  10.1 2.5 %collective-permute-done.1 = bf16[4,128,128]{2,1,0:T(8,128)(2,1)S(1)} collective-permute-done((bf16[4,128,128]{2,1,0:T(8,128)(2,1)S(1)}, bf16[4,128,128]{2,1,0:T(8,128)(2,1)S(1)}, u32[]{:S(2)}, u32[]{:S(2)}) %collective-permute-start.1) | collective-permute-done | bytes 131104 | tf_op jit(solution)/shard_map/ppermute | solution.py:141
  12.6 2.9 %collective-permute-start.2 = (bf16[4,128,128]{2,1,0:T(8,128)(2,1)S(1)}, bf16[4,128,128]{2,1,0:T(8,128)(2,1)S(1)}, u32[]{:S(2)}, u32[]{:S(2)}) collective-permute-start(bf16[4,128,128]{2,1,0:T(8,128)(2,1)S(1)} %broadcast_select_fusion), channel_id=1, source_target_pairs={{0,8},{1,9},{2,10},{3,11},{4,12},{5,13},{6,14},{7,15},{8,0},{9,1},... | collective-permute-start | bytes 393224 | tf_op jit(solution)/shard_map/ppermute | solution.py:141
  15.5 0.6 %add_add_fusion.scalars = s32[3]{0:T(128)} fusion(s32[1]{0:T(128)} %bitcast, s32[1]{0:T(128)} %bitcast.2, s32[1]{0:T(128)S(6)} %copy.12), kind=kLoop, calls=%fused_computation.8 | loop fusion | flops 6 | bytes 24 | tf_op jit(solution)/shard_map/stack | solution.py:155
  16.1 2.3 %shard_map.109 = (bf16[8,128,128]{2,1,0:T(8,128)(2,1)}, f32[8,16,128]{2,1,0:T(8,128)}) custom-call(s32[3]{0:T(128)} %add_add_fusion.scalars, bf16[8,128,128]{2,1,0:T(8,128)(2,1)} %x_ref.1, f32[1,128]{1,0:T(1,128)} %bitcast.22, bf16[128,128]{1,0:T(8,128)(2,1)} %w_ref.2, bf16[128,128]{1,0:T(8,128)(2,1)} %wg_ref.2, bf16[128,128]{1,0:T(8,128)(2,1)} %wo_ref.1), custom_call_target="tpu_custom_call" | custom-call | tf_op jit(solution)/shard_map/pallas_call | solution.py:148
  18.4 0.6 %add_add_fusion.1.scalars = s32[3]{0:T(128)} fusion(s32[1]{0:T(128)} %bitcast.7, s32[1]{0:T(128)} %bitcast.2, s32[1]{0:T(128)S(6)} %copy.12), kind=kLoop, calls=%fused_computation.9 | loop fusion | flops 6 | bytes 24 | tf_op jit(solution)/shard_map/stack | solution.py:165
  18.9 1.0 %collective-permute-done.2 = bf16[4,128,128]{2,1,0:T(8,128)(2,1)S(1)} collective-permute-done((bf16[4,128,128]{2,1,0:T(8,128)(2,1)S(1)}, bf16[4,128,128]{2,1,0:T(8,128)(2,1)S(1)}, u32[]{:S(2)}, u32[]{:S(2)}) %collective-permute-start.2) | collective-permute-done | bytes 131104 | tf_op jit(solution)/shard_map/ppermute | solution.py:141
  19.9 0.7 %broadcast_select_fusion.1.x_ref = bf16[4,128,128]{2,1,0:T(8,128)(2,1)} fusion(bf16[4,128,128]{2,1,0:T(8,128)(2,1)S(1)} %broadcast_select_fusion, bf16[4,128,128]{2,1,0:T(8,128)(2,1)S(1)} %collective-permute-done.2, pred[]{:T(512)S(6)} %eq.22), kind=kLoop, calls=%fused_computation.3 | loop fusion | flops 65536 | bytes 393217 | tf_op jit(solution)/shard_map/jit(_where)/select_n | solution.py:159
  20.6 0.0 copy-start.5
  20.6 2.0 %shard_map.110.refs_0_ = bf16[4,128,128]{2,1,0:T(8,128)(2,1)} custom-call(s32[3]{0:T(128)} %add_add_fusion.1.scalars, bf16[4,128,128]{2,1,0:T(8,128)(2,1)} %broadcast_select_fusion.1.x_ref, f32[1,128]{1,0:T(1,128)} %bitcast.23, bf16[128,128]{1,0:T(8,128)(2,1)} %w_ref.3, bf16[128,128]{1,0:T(8,128)(2,1)} %wg_ref.3), custom_call_target="tpu_custom_call" | custom-call | tf_op jit(solution)/shard_map/pallas_call | solution.py:163
  22.6 0.0 copy-start.1
  22.6 1.7 %collective-permute-start.3 = (bf16[4,128,128]{2,1,0:T(8,128)(2,1)}, bf16[4,128,128]{2,1,0:T(8,128)(2,1)S(1)}, u32[]{:S(2)}, u32[]{:S(2)}) collective-permute-start(bf16[4,128,128]{2,1,0:T(8,128)(2,1)} %shard_map.110.refs_0_), channel_id=1, source_target_pairs={{0,2},{1,3},{2,0},{3,1},{4,6},{5,7},{6,4},{7,5},{8,10},{9,11},{10,... | collective-permute-start | bytes 393224 | tf_op jit(solution)/shard_map/ppermute | solution.py:141
  24.4 0.0 copy-done.5
  24.4 0.0 copy-done.1
  24.4 0.1 collective-permute-start.4
  24.5 3.3 %collective-permute-done.3.refs_1_ = bf16[4,128,128]{2,1,0:T(8,128)(2,1)S(1)} collective-permute-done((bf16[4,128,128]{2,1,0:T(8,128)(2,1)}, bf16[4,128,128]{2,1,0:T(8,128)(2,1)S(1)}, u32[]{:S(2)}, u32[]{:S(2)}) %collective-permute-start.3) | collective-permute-done | bytes 131104 | tf_op jit(solution)/shard_map/ppermute | solution.py:141
  27.8 0.0 copy-start.2
  27.8 0.0 collective-permute-start.5
  27.8 0.7 %reverse_select_fusion = f32[8,2,2,4,128]{4,3,2,1,0:T(4,128)} fusion(f32[8,2,2,4,128]{4,3,2,1,0:T(4,128)S(1)} %reverse_select_fusion.1, pred[]{:T(512)S(6)} %eq.20), kind=kLoop, calls=%fused_computation.4 | loop fusion | flops 16384 | bytes 131073 | tf_op jit(solution)/shard_map/jit(_where)/select_n | solution.py:180
  28.5 0.0 collective-permute-done.4.refs_2_
  28.5 0.0 copy-start.3
  28.5 0.7 %collective-permute-done.5.refs_3_ = bf16[4,128,128]{2,1,0:T(8,128)(2,1)S(1)} collective-permute-done((bf16[4,128,128]{2,1,0:T(8,128)(2,1)S(1)}, bf16[4,128,128]{2,1,0:T(8,128)(2,1)S(1)}, u32[]{:S(2)}, u32[]{:S(2)}) %collective-permute-start.5) | collective-permute-done | bytes 131104 | tf_op jit(solution)/shard_map/ppermute | solution.py:141
  29.2 0.0 copy-start.4
  29.2 0.0 copy-done.2
  29.2 0.0 copy-done.3
  29.2 0.6 %copy-done.4 = bf16[4,128,128]{2,1,0:T(8,128)(2,1)} copy-done((bf16[4,128,128]{2,1,0:T(8,128)(2,1)}, bf16[4,128,128]{2,1,0:T(8,128)(2,1)S(1)}, u32[]{:S(2)}) %copy-start.4) | copy-done | bytes 131096
  29.8 2.9 %shard_map.111 = bf16[8,16,128]{2,1,0:T(8,128)(2,1)} custom-call(bf16[8,128,128]{2,1,0:T(8,128)(2,1)} %get-tuple-element.7.left_ref, f32[8,16,128]{2,1,0:T(8,128)} %bitcast.19, bf16[128,128]{1,0:T(8,128)(2,1)} %w_out_ref.1, f32[1,128]{1,0:T(1,128)} %bitcast.24, bf16[4,128,128]{2,1,0:T(8,128)(2,1)} %shard_map.110.refs_0_, bf16[4,128,128]{2,1,0:T(8,128)(2,1)} %copy-done.2, ...), custom_call_target="tpu_custom_call" | custom-call | tf_op jit(solution)/shard_map/pallas_call | solution.py:185
  32.7 0.9 %reverse_select_fusion.3 = bf16[8,2,2,4,128]{4,3,2,1,0:T(4,128)(2,1)S(1)} fusion(bf16[8,2,2,4,128]{4,3,2,1,0:T(4,128)(2,1)} %bitcast.20, pred[]{:T(512)S(6)} %eq.21), kind=kLoop, calls=%fused_computation.7 | loop fusion | flops 16384 | bytes 65537 | tf_op jit(solution)/shard_map/jit(_where)/select_n | solution.py:176
  33.5 0.6 %reverse_select_fusion.2 = bf16[8,2,2,4,128]{4,3,2,1,0:T(4,128)(2,1)} fusion(bf16[8,2,2,4,128]{4,3,2,1,0:T(4,128)(2,1)S(1)} %reverse_select_fusion.3, pred[]{:T(512)S(6)} %eq.20), kind=kLoop, calls=%fused_computation.6 | loop fusion | flops 16384 | bytes 65537 | tf_op jit(solution)/shard_map/jit(_where)/select_n | solution.py:180
  (3 shorter events, 0.0 us)
Async XLA Ops:
  0.0 7.5 %copy-start = (bf16[8,128,128]{2,1,0:T(8,128)(2,1)S(1)}, bf16[8,128,128]{2,1,0:T(8,128)(2,1)}, u32[]{:S(2)}) copy-start(bf16[8,128,128]{2,1,0:T(8,128)(2,1)} %x_ref.1) | copy-start | bytes 786436
  1.0 6.5 %collective-permute-start = (bf16[4,128,128]{2,1,0:T(8,128)(2,1)S(1)}, bf16[4,128,128]{2,1,0:T(8,128)(2,1)S(1)}, u32[]{:S(2)}, u32[]{:S(2)}) collective-permute-start(bf16[4,128,128]{2,1,0:T(8,128)(2,1)S(1)} %dynamic-slice_bitcast_fusion), channel_id=1, source_target_pairs={{0,2},{1,3},{2,0},{3,1},{4,6},{5,7},{6,4},{7,5},{8,10},{9,11},{10,... | collective-permute-start | bytes 393224 | tf_op jit(solution)/shard_map/ppermute | solution.py:141
  7.5 5.0 %collective-permute-start.1 = (bf16[4,128,128]{2,1,0:T(8,128)(2,1)S(1)}, bf16[4,128,128]{2,1,0:T(8,128)(2,1)S(1)}, u32[]{:S(2)}, u32[]{:S(2)}) collective-permute-start(bf16[4,128,128]{2,1,0:T(8,128)(2,1)S(1)} %bitcast_select_fusion), channel_id=1, source_target_pairs={{0,4},{1,5},{2,6},{3,7},{4,0},{5,1},{6,2},{7,3},{8,12},{9,13},{10,... | collective-permute-start | bytes 393224 | tf_op jit(solution)/shard_map/ppermute | solution.py:141
  12.6 7.3 %collective-permute-start.2 = (bf16[4,128,128]{2,1,0:T(8,128)(2,1)S(1)}, bf16[4,128,128]{2,1,0:T(8,128)(2,1)S(1)}, u32[]{:S(2)}, u32[]{:S(2)}) collective-permute-start(bf16[4,128,128]{2,1,0:T(8,128)(2,1)S(1)} %broadcast_select_fusion), channel_id=1, source_target_pairs={{0,8},{1,9},{2,10},{3,11},{4,12},{5,13},{6,14},{7,15},{8,0},{9,1},... | collective-permute-start | bytes 393224 | tf_op jit(solution)/shard_map/ppermute | solution.py:141
  20.6 3.8 %copy-start.5 = (f32[8,16,128]{2,1,0:T(8,128)S(1)}, f32[8,16,128]{2,1,0:T(8,128)}, u32[]{:S(2)}) copy-start(f32[8,16,128]{2,1,0:T(8,128)} %get-tuple-element.8) | copy-start | bytes 196612
  22.6 1.8 %copy-start.1 = (bf16[4,128,128]{2,1,0:T(8,128)(2,1)S(1)}, bf16[4,128,128]{2,1,0:T(8,128)(2,1)}, u32[]{:S(2)}) copy-start(bf16[4,128,128]{2,1,0:T(8,128)(2,1)} %shard_map.110.refs_0_) | copy-start | bytes 393220
  22.6 5.2 %collective-permute-start.3 = (bf16[4,128,128]{2,1,0:T(8,128)(2,1)}, bf16[4,128,128]{2,1,0:T(8,128)(2,1)S(1)}, u32[]{:S(2)}, u32[]{:S(2)}) collective-permute-start(bf16[4,128,128]{2,1,0:T(8,128)(2,1)} %shard_map.110.refs_0_), channel_id=1, source_target_pairs={{0,2},{1,3},{2,0},{3,1},{4,6},{5,7},{6,4},{7,5},{8,10},{9,11},{10,... | collective-permute-start | bytes 393224 | tf_op jit(solution)/shard_map/ppermute | solution.py:141
  24.4 4.1 %collective-permute-start.4 = (bf16[4,128,128]{2,1,0:T(8,128)(2,1)S(1)}, bf16[4,128,128]{2,1,0:T(8,128)(2,1)S(1)}, u32[]{:S(2)}, u32[]{:S(2)}) collective-permute-start(bf16[4,128,128]{2,1,0:T(8,128)(2,1)S(1)} %copy-done.1), channel_id=1, source_target_pairs={{0,1},{1,0},{2,3},{3,2},{4,5},{5,4},{6,7},{7,6},{8,9},{9,8},{10,11... | collective-permute-start | bytes 393224 | tf_op jit(solution)/shard_map/ppermute | solution.py:141
  27.8 1.4 %copy-start.2 = (bf16[4,128,128]{2,1,0:T(8,128)(2,1)}, bf16[4,128,128]{2,1,0:T(8,128)(2,1)S(1)}, u32[]{:S(2)}) copy-start(bf16[4,128,128]{2,1,0:T(8,128)(2,1)S(1)} %collective-permute-done.3.refs_1_) | copy-start | bytes 393220
  27.8 1.3 %collective-permute-start.5 = (bf16[4,128,128]{2,1,0:T(8,128)(2,1)S(1)}, bf16[4,128,128]{2,1,0:T(8,128)(2,1)S(1)}, u32[]{:S(2)}, u32[]{:S(2)}) collective-permute-start(bf16[4,128,128]{2,1,0:T(8,128)(2,1)S(1)} %collective-permute-done.3.refs_1_), channel_id=1, source_target_pairs={{0,1},{1,0},{2,3},{3,2},{4,5},{5,4},{6,7},{7,6},{8,9},{9,8},{10,11... | collective-permute-start | bytes 393224 | tf_op jit(solution)/shard_map/ppermute | solution.py:141
  28.5 0.7 %copy-start.3 = (bf16[4,128,128]{2,1,0:T(8,128)(2,1)}, bf16[4,128,128]{2,1,0:T(8,128)(2,1)S(1)}, u32[]{:S(2)}) copy-start(bf16[4,128,128]{2,1,0:T(8,128)(2,1)S(1)} %collective-permute-done.4.refs_2_) | copy-start | bytes 393220
  29.2 0.7 %copy-start.4 = (bf16[4,128,128]{2,1,0:T(8,128)(2,1)}, bf16[4,128,128]{2,1,0:T(8,128)(2,1)S(1)}, u32[]{:S(2)}) copy-start(bf16[4,128,128]{2,1,0:T(8,128)(2,1)S(1)} %collective-permute-done.5.refs_3_) | copy-start | bytes 393220

commit v2 on v1

v2 whole, which is shorter than its diff:
```python
import functools

import jax
import jax.numpy as jnp
from jax import lax
from jax.experimental import pallas as pl
from jax.experimental.pallas import tpu as pltpu
from jax.sharding import PartitionSpec as P

BLOCKS = 8
QUAD = 4
GROUPS = ((0, 1, 2, 3), (4, 5, 6, 7))
VMEM = pl.BlockSpec(memory_space=pltpu.VMEM)


def sigmoid(values):
    return 0.5 * jnp.tanh(0.5 * values) + 0.5


def layer_norm(values, gain):
    scale = 1.0 / values.shape[-1]
    mean_v = jnp.sum(values, axis=-1, keepdims=True) * scale
    centered = values - mean_v
    variance_v = jnp.sum(centered * centered, axis=-1, keepdims=True) * scale
    return centered * lax.rsqrt(variance_v + 1e-05) * gain


def dot(left, right):
    return jnp.dot(left, right, preferred_element_type=jnp.float32)


def scalar(ref, slot):
    return ref[0:1, slot : slot + 1][0, 0]


def steps(count, body):
    if count <= 16:
        for step in range(count):
            body(step)
    else:
        pl.loop(0, count)(body)


def edge_rows(chunk, first, valid, read, gain_ref, w_ref, wg_ref, out_ref):
    rows, tokens, _ = out_ref.shape
    per_row = tokens // chunk
    gain = gain_ref[...]
    ids = lax.broadcasted_iota(jnp.int32, (chunk, 1), 0)

    def body(step):
        row, col = step // per_row, (step % per_row) * chunk
        here = jnp.logical_and(first + row < valid, ids + col < valid)
        normed = layer_norm(read(row, pl.ds(col, chunk)).astype(jnp.float32), gain).astype(jnp.bfloat16)
        edge = sigmoid(dot(normed, wg_ref[...])) * dot(normed, w_ref[...]) * here.astype(jnp.float32)
        out_ref[row, pl.ds(col, chunk), :] = edge.astype(jnp.bfloat16).astype(out_ref.dtype)

    steps(rows * per_row, body)


def left_body(chunk, scalars, x_ref, gain_ref, w_ref, wg_ref, wo_ref, out_ref, gate_ref):
    edge_rows(
        chunk, scalar(scalars, 1), scalar(scalars, 0), lambda row, at: x_ref[row, at, :], gain_ref, w_ref, wg_ref, out_ref
    )
    rows, width, channels = gate_ref.shape
    at = pl.ds(pl.multiple_of(scalar(scalars, 2), width), width)
    gain = gain_ref[...]

    def body(row):
        normed = layer_norm(x_ref[row, at, :].astype(jnp.float32), gain).astype(jnp.bfloat16)
        gate_ref[row] = sigmoid(dot(normed, wo_ref[...]))

    steps(rows, body)


def right_body(chunk, scalars, *refs):
    candidates, (gain_ref, w_ref, wg_ref, out_ref) = refs[:-4], refs[-4:]
    which = scalar(scalars, 4)

    def read(row, at):
        value = candidates[0][row, at, :]
        for d in range(1, len(candidates)):
            value = jnp.where(which == d, candidates[d][row, at, :], value)
        return value

    edge_rows(chunk, scalar(scalars, 3), scalar(scalars, 0), read, gain_ref, w_ref, wg_ref, out_ref)


def contract(places, small, which, part, left_ref, right_ref, lanes, store):
    rows, tokens, channels = left_ref.shape
    depth = min(tokens, 128)
    for at_piece, (p, d) in enumerate(places):
        base = (part ^ p) * rows + (which ^ d) * small

        def over(k, first, at_piece=at_piece):
            at = pl.ds(k * depth, depth)
            rights = [
                right_ref[at_piece * small + t, at, :].astype(jnp.float32).reshape(-1, 8, channels)
                for t in range(small)
            ]
            for i in range(rows):
                l = left_ref[i, at, :].reshape(-1, 8, channels)
                for t in range(small):
                    here = pl.ds((t * rows + i) * 8, 8)
                    total = jnp.sum(l * rights[t], axis=0)
                    lanes[here, :] = total if first else lanes[here, :] + total

        over(0, True)
        if tokens > depth:
            pl.loop(1, tokens // depth)(lambda k: over(k, False))
        for t in range(small):
            total = lanes[pl.ds(t * rows * 8, rows, stride=8), :]
            for s in range(1, 8):
                total = total + lanes[pl.ds(t * rows * 8 + s, rows, stride=8), :]
            store(base + t, at_piece * small + t, total)


def early_body(order, small, scalars, left_ref, *refs):
    right_refs, out_ref, lanes = refs[:-2], refs[-2], refs[-1]
    at_row = 0
    for right_ref, places in zip(right_refs, order):

        def store(j, held_at, total, at_row=at_row):
            out_ref[at_row + held_at] = total

        contract(places, small, scalar(scalars, 4), scalar(scalars, 5), left_ref, right_ref, lanes, store)
        at_row += right_ref.shape[0]


def finish_body(early_order, n_early, order, small, scalars, left_ref, gate_ref, w_out_ref, gain_ref, *refs):
    out_ref, product, result, lanes = refs[-4:]
    rows, tokens, channels = left_ref.shape
    width = out_ref.shape[1]
    which, part = scalar(scalars, 4), scalar(scalars, 5)
    right_refs = refs[:-4]
    early_rows = [ref.at[t] for ref in right_refs[:n_early] for t in range(ref.shape[0])]
    right_refs = right_refs[n_early:]
    for at_piece, (p, d) in enumerate(sum(early_order, [])):
        for t in range(small):
            product[(part ^ p) * rows + (which ^ d) * small + t] = early_rows[at_piece * small + t][...]

    def store(j, held_at, total):
        product[j] = total

    for right_ref, places in zip(right_refs, order):
        contract(places, small, which, part, left_ref, right_ref, lanes, store)
    normed = layer_norm(product[...].reshape(width * rows, channels), gain_ref[...]).astype(jnp.bfloat16)
    result[...] = dot(normed, w_out_ref[...])
    for i in range(rows):
        out_ref[i] = (gate_ref[i] * result[pl.ds(i, width, stride=rows), :]).astype(jnp.bfloat16)


def prepare_body(rows, width, gain_ref, later_ref, valid_ref, window_ref, gain_out, later_out, numbers_ref):
    gain_out[...] = gain_ref[...]
    later_out[...] = later_ref[...]
    small, parts = rows // QUAD, width // rows
    me = lax.axis_index("row").astype(jnp.int32)
    block, part = lax.div(me, parts), lax.rem(me, parts)
    window = window_ref[...]
    which = (window ^ block) & (QUAD - 1)
    start = window * width
    at = lax.broadcasted_iota(jnp.int32, numbers_ref.shape, 1)
    values = [valid_ref[...], me * rows, start, start + part * rows + which * small, which, part]
    numbers = jnp.zeros(numbers_ref.shape, jnp.int32)
    for slot, value in enumerate(values):
        numbers = jnp.where(at == slot, value, numbers)
    numbers_ref[...] = numbers


def size(values):
    return values.size * values.dtype.itemsize


def local(body, out_shape, scalars, *operands, scratch=()):
    outs = jax.tree.leaves(out_shape)
    need = sum(size(v) for v in operands) + sum(size(v) for v in outs)
    return pl.pallas_call(
        body,
        out_shape=out_shape,
        in_specs=[VMEM] * (1 + len(operands)),
        out_specs=jax.tree.map(lambda _: VMEM, out_shape),
        scratch_shapes=list(scratch),
        compiler_params=pltpu.CompilerParams(vmem_limit_bytes=min(60 * 2**20, 2 * need + 8 * 2**20)),
    )(scalars, *operands)


def on_device(
    pair_rows, in_gain, w_left, w_left_gate, w_right, w_right_gate, w_gate, w_out, out_gain, valid_len, window, devices
):
    rows, tokens, channels = pair_rows.shape
    width = tokens // BLOCKS
    parts = width // rows
    small = rows // QUAD
    chunk = min(tokens, 128)
    bf16, f32 = jnp.bfloat16, jnp.float32
    differs = lax.div(lax.axis_index("row").astype(jnp.int32), parts) ^ window[0]
    gain_shape = jax.ShapeDtypeStruct((1, channels), f32)
    in_gain, out_gain, scalars = pl.pallas_call(
        functools.partial(prepare_body, rows, width),
        out_shape=(gain_shape, gain_shape, jax.ShapeDtypeStruct((1, 128), jnp.int32)),
        in_specs=[VMEM] * 4,
        out_specs=(VMEM,) * 3,
        compiler_params=pltpu.CompilerParams(vmem_limit_bytes=8 * 2**20),
    )(in_gain.reshape(1, channels), out_gain.reshape(1, channels), valid_len.reshape(1, 1), window.reshape(1, 1))

    def swap(values, mask):
        return lax.ppermute(values, "row", [(i, i ^ mask) for i in range(devices)])

    got = {d: swap(pair_rows[d * small : (d + 1) * small], parts * d) for d in reversed(range(1, QUAD))}
    right = local(
        functools.partial(right_body, chunk),
        jax.ShapeDtypeStruct((small, tokens, channels), bf16),
        scalars, pair_rows[:small], *[got[d] for d in range(1, QUAD)], in_gain, w_right, w_right_gate,
    )
    left, gate = local(
        functools.partial(left_body, chunk),
        (
            jax.ShapeDtypeStruct((rows, tokens, channels), f32),
            jax.ShapeDtypeStruct((rows, width, channels), f32),
        ),
        scalars, pair_rows, in_gain, w_left, w_left_gate, w_gate,
    )
    bit = QUAD
    while bit < BLOCKS:
        other, left = lax.optimization_barrier((swap(right, parts * bit), left))
        right = jnp.where(differs & bit == 0, right, other)
        bit *= 2

    held, order = [right], [[(0, 0)]]
    for d in reversed(range(1, QUAD)):
        held.append(swap(right, parts * d))
        order.append([(0, d)])
    bit = 1
    while bit < parts:
        if bit > 1:
            held, order = [jnp.concatenate(held)], [sum(order, [])]
        held = held + [swap(values, bit) for values in held]
        order = order + [[(p ^ bit, d) for p, d in places] for places in order]
        bit *= 2

    lanes = pltpu.VMEM((small * rows * 8, channels), f32)
    groups = GROUPS if len(held) == 8 else (range(len(held)),)
    early, early_order = [], []
    for group in groups[:-1]:
        chosen = [order[i] for i in group]
        early_order += chosen
        early.append(
            local(
                functools.partial(early_body, chosen, small),
                jax.ShapeDtypeStruct((sum(held[i].shape[0] for i in group), rows, channels), f32),
                scalars, left, *[held[i] for i in group],
                scratch=[lanes],
            )
        )
    late_order = [order[i] for i in groups[-1]]
    late = [held[i] for i in groups[-1]]
    return local(
        functools.partial(finish_body, early_order, len(early), late_order, small),
        jax.ShapeDtypeStruct((rows, width, channels), bf16),
        scalars, left, gate, w_out, out_gain, *early, *late,
        scratch=[pltpu.VMEM((width, rows, channels), f32), pltpu.VMEM((width * rows, channels), f32), lanes],
    )


def solution(mesh):
    return jax.shard_map(
        functools.partial(on_device, devices=mesh.shape["row"]),
        mesh=mesh,
        in_specs=(P(("groups", "row"), None, None),) + (P(),) * 8 + (P("groups"),) * 2,
        out_specs=P(("groups", "row"), None, None),
        check_vma=False,
    )
```

time: 34.5 us -> 26.3 us (0.76)
  Pallas kernels: 7.19 us -> 2.92 us
  other arithmetic: 4.04 us -> 0.01 us
  starting transfers between devices: 9.58 us -> 11.4 us
  waiting for transfers between devices: 10.3 us -> 9.4 us
  local copies, waits for them, and re-layouts: 1.65 us -> 1.03 us
    pallas_call x3 -> x5, Pallas kernels: 7.19 us -> 2.92 us  [the longest x4 2.83 us: local(): pl.pallas_call(body, out_shape=out_shape, in_specs=[VMEM] * (1 + len(oper...]
    select_n x7 -> x1, other arithmetic: 2.87 us -> 0.01 us  [on_device(): right = jnp.where(differs & bit == 0, right, other)]
    ppermute x6 -> x11, starting transfers between devices: 9.58 us -> 11.4 us  [swap(): return lax.ppermute(values, 'row', [(i, i ^ mask) for i in range(devices)])]
    another operation x2 -> x0, other arithmetic: 1.17 us -> none  [the longest x1 0.61 us: on_device(): jnp.stack([valid, me * rows, start])]
    slice x0 -> x1, local copies, waits for them, and re-layouts: none -> 0.99 us  [on_device(): pair_rows[d * small:(d + 1) * small]]
    squeeze x1 -> x0, local copies, waits for them, and re-layouts: 0.99 us -> none  [on_device(): sent = lax.dynamic_index_in_dim(halves, 1 - sub, 0, keepdims=False)]
    ppermute x6 -> x11, waiting for transfers between devices: 10.3 us -> 9.4 us  [swap(): return lax.ppermute(values, 'row', [(i, i ^ mask) for i in range(devices)])]
    unnamed x12 -> x18, local copies, waits for them, and re-layouts: 0.66 us -> 0.04 us
  transfers between devices with their start and end apart: 6 -> 11, of which waited for: 5 -> 6; matrix products, arithmetic and copies ran while one was open for 5% -> 0% of each run, Pallas kernels for 7% -> 4%
where the time goes in v2:
time: 26.3 us; the launch traced here: 26.1 us
  starting transfers between devices  11.4 us (43%)
  waiting for transfers between devices  9.4 us (36%)
  Pallas kernels  2.92 us (11%)
  between operations  1.41 us (5%)
  local copies, waits for them, and re-layouts  1.03 us (4%)
    ppermute x11, starting transfers between devices, swap(): return lax.ppermute(values, 'row', [(i, i ^ mask) for i in range(devices)])  11.4 us
    ppermute x11, waiting for transfers between devices, swap(): return lax.ppermute(values, 'row', [(i, i ^ mask) for i in range(devices)])  9.4 us
    pallas_call x4, Pallas kernels, local(): pl.pallas_call(body, out_shape=out_shape, in_specs=[VMEM] * (1 + len(oper...  2.83 us
    slice x1, local copies, waits for them, and re-layouts, on_device(): pair_rows[d * small:(d + 1) * small]  0.99 us
  transfers between devices with their start and end apart: 11, of which 6 were waited for; matrix products, arithmetic and copies ran while one was open for 0% of the time, Pallas kernels for 4%

profile of v2, /device:TPU:0, one launch (start us, length us, event | category | flops | bytes accessed | tf_op | source)
XLA Modules:
  0.0 26.1 jit_solution(16486512845050530650)
XLA Ops:
  0.0 0.0 copy-start.7
  0.0 0.0 copy-start.8
  0.0 0.0 copy-start.1
  0.0 0.0 copy-start.2
  0.0 1.0 %fusion = (bf16[2,128,128]{2,1,0:T(8,128)(2,1)S(1)}, bf16[2,128,128]{2,1,0:T(8,128)(2,1)S(1)}, bf16[2,128,128]{2,1,0:T(8,128)(2,1)S(1)}, bf16[2,128,128]{2,1,0:T(8,128)(2,1)S(1)}) fusion(bf16[8,128,128]{2,1,0:T(8,128)(2,1)} %x_ref.1), kind=kLoop, calls=%fused_computation.1 | loop fusion | bytes 524288 | tf_op jit(solution)/shard_map/slice | solution.py:208
  1.0 0.0 copy-start
  1.0 3.1 %collective-permute-start = (bf16[2,128,128]{2,1,0:T(8,128)(2,1)S(1)}, bf16[2,128,128]{2,1,0:T(8,128)(2,1)S(1)}, u32[]{:S(2)}, u32[]{:S(2)}) collective-permute-start(bf16[2,128,128]{2,1,0:T(8,128)(2,1)S(1)} %get-tuple-element.21), channel_id=1, source_target_pairs={{0,2},{1,3},{2,0},{3,1},{4,6},{5,7},{6,4},{7,5},{8,10},{9,11},{10,... | collective-permute-start | bytes 196616 | tf_op jit(solution)/shard_map/ppermute | solution.py:206
  4.1 1.6 %collective-permute-start.1 = (bf16[2,128,128]{2,1,0:T(8,128)(2,1)S(1)}, bf16[2,128,128]{2,1,0:T(8,128)(2,1)S(1)}, u32[]{:S(2)}, u32[]{:S(2)}) collective-permute-start(bf16[2,128,128]{2,1,0:T(8,128)(2,1)S(1)} %get-tuple-element.20), channel_id=1, source_target_pairs={{0,4},{1,5},{2,6},{3,7},{4,0},{5,1},{6,2},{7,3},{8,12},{9,13},{10,... | collective-permute-start | bytes 196616 | tf_op jit(solution)/shard_map/ppermute | solution.py:206
  5.6 0.0 collective-permute-start.2
  6.9 0.0 copy-done.7
  7.0 0.0 copy-done.8
  7.0 0.1 shard_map.109
  7.0 0.0 collective-permute-done.refs_1_
  7.1 1.8 %collective-permute-done.1.refs_2_ = bf16[2,128,128]{2,1,0:T(8,128)(2,1)S(1)} collective-permute-done((bf16[2,128,128]{2,1,0:T(8,128)(2,1)S(1)}, bf16[2,128,128]{2,1,0:T(8,128)(2,1)S(1)}, u32[]{:S(2)}, u32[]{:S(2)}) %collective-permute-start.1) | collective-permute-done | bytes 65568 | tf_op jit(solution)/shard_map/ppermute | solution.py:206
  8.9 1.9 %collective-permute-done.2.refs_3_ = bf16[2,128,128]{2,1,0:T(8,128)(2,1)S(1)} collective-permute-done((bf16[2,128,128]{2,1,0:T(8,128)(2,1)S(1)}, bf16[2,128,128]{2,1,0:T(8,128)(2,1)S(1)}, u32[]{:S(2)}, u32[]{:S(2)}) %collective-permute-start.2) | collective-permute-done | bytes 65568 | tf_op jit(solution)/shard_map/ppermute | solution.py:206
  10.8 0.0 copy-done.1
  10.8 0.0 copy-done.2
  10.8 0.0 copy-start.4
  10.8 0.0 copy-start.5
  10.8 0.0 copy-start.6
  10.8 0.4 %shard_map.110 = bf16[2,128,128]{2,1,0:T(8,128)(2,1)S(1)} custom-call(s32[1,128]{1,0:T(1,128)S(1)} %get-tuple-element.12.scalars, bf16[2,128,128]{2,1,0:T(8,128)(2,1)S(1)} %get-tuple-element.22.refs_0_, bf16[2,128,128]{2,1,0:T(8,128)(2,1)S(1)} %collective-permute-done.refs_1_, bf16[2,128,128]{2,1,0:T(8,128)(2,1)S(1)} %collective-permute-done.1.refs_2_, ...), custom_call_target="tpu_custom_call" | custom-call | tf_op jit(solution)/shard_map/pallas_call | solution.py:176
  11.3 2.7 %collective-permute-start.3 = (bf16[2,128,128]{2,1,0:T(8,128)(2,1)S(1)}, bf16[2,128,128]{2,1,0:T(8,128)(2,1)S(1)}, u32[]{:S(2)}, u32[]{:S(2)}) collective-permute-start(bf16[2,128,128]{2,1,0:T(8,128)(2,1)S(1)} %shard_map.110), channel_id=1, source_target_pairs={{0,8},{1,9},{2,10},{3,11},{4,12},{5,13},{6,14},{7,15},{8,0},{9,1},... | collective-permute-start | bytes 196616 | tf_op jit(solution)/shard_map/ppermute | solution.py:206
  13.9 0.0 copy-done
  13.9 0.0 copy-done.4
  13.9 0.0 copy-done.5
  13.9 0.0 copy-done.6
  14.0 0.7 %shard_map.111 = (f32[8,128,128]{2,1,0:T(8,128)S(1)}, f32[8,16,128]{2,1,0:T(8,128)S(1)}) custom-call(s32[1,128]{1,0:T(1,128)S(1)} %get-tuple-element.12.scalars, bf16[8,128,128]{2,1,0:T(8,128)(2,1)S(1)} %copy-done, f32[1,128]{1,0:T(1,128)S(1)} %get-tuple-element.13.refs_4_.gain_ref, bf16[128,128]{1,0:T(8,128)(2,1)S(1)} %copy-done.4, ...), custom_call_target="tpu_custom_call" | custom-call | tf_op jit(solution)/shard_map/pallas_call | solution.py:176
  14.7 2.4 %collective-permute-done.3 = bf16[2,128,128]{2,1,0:T(8,128)(2,1)S(1)} collective-permute-done((bf16[2,128,128]{2,1,0:T(8,128)(2,1)S(1)}, bf16[2,128,128]{2,1,0:T(8,128)(2,1)S(1)}, u32[]{:S(2)}, u32[]{:S(2)}) %collective-permute-start.3) | collective-permute-done | bytes 65568 | tf_op jit(solution)/shard_map/ppermute | solution.py:206
  17.1 0.0 copy-start.3
  17.1 0.3 %collective-permute-start.4 = (bf16[2,128,128]{2,1,0:T(8,128)(2,1)S(1)}, bf16[2,128,128]{2,1,0:T(8,128)(2,1)S(1)}, u32[]{:S(2)}, u32[]{:S(2)}) collective-permute-start(bf16[2,128,128]{2,1,0:T(8,128)(2,1)S(1)} %broadcast_select_fusion.refs_0_), channel_id=1, source_target_pairs={{0,6},{1,7},{2,4},{3,5},{4,2},{5,3},{6,0},{7,1},{8,14},{9,15},{10,... | collective-permute-start | bytes 196616 | tf_op jit(solution)/shard_map/ppermute | solution.py:206
  17.4 1.9 %collective-permute-start.5 = (bf16[2,128,128]{2,1,0:T(8,128)(2,1)S(1)}, bf16[2,128,128]{2,1,0:T(8,128)(2,1)S(1)}, u32[]{:S(2)}, u32[]{:S(2)}) collective-permute-start(bf16[2,128,128]{2,1,0:T(8,128)(2,1)S(1)} %broadcast_select_fusion.refs_0_), channel_id=1, source_target_pairs={{0,4},{1,5},{2,6},{3,7},{4,0},{5,1},{6,2},{7,3},{8,12},{9,13},{10,... | collective-permute-start | bytes 196616 | tf_op jit(solution)/shard_map/ppermute | solution.py:206
  19.3 1.4 %collective-permute-start.6 = (bf16[2,128,128]{2,1,0:T(8,128)(2,1)S(1)}, bf16[2,128,128]{2,1,0:T(8,128)(2,1)S(1)}, u32[]{:S(2)}, u32[]{:S(2)}) collective-permute-start(bf16[2,128,128]{2,1,0:T(8,128)(2,1)S(1)} %broadcast_select_fusion.refs_0_), channel_id=1, source_target_pairs={{0,2},{1,3},{2,0},{3,1},{4,6},{5,7},{6,4},{7,5},{8,10},{9,11},{10,... | collective-permute-start | bytes 196616 | tf_op jit(solution)/shard_map/ppermute | solution.py:206
  20.7 0.0 collective-permute-start.7
  20.7 1.7 %collective-permute-done.4.refs_1_ = bf16[2,128,128]{2,1,0:T(8,128)(2,1)S(1)} collective-permute-done((bf16[2,128,128]{2,1,0:T(8,128)(2,1)S(1)}, bf16[2,128,128]{2,1,0:T(8,128)(2,1)S(1)}, u32[]{:S(2)}, u32[]{:S(2)}) %collective-permute-start.4) | collective-permute-done | bytes 65568 | tf_op jit(solution)/shard_map/ppermute | solution.py:206
  22.4 0.0 collective-permute-start.8
  22.4 0.0 collective-permute-done.5.refs_2_
  22.4 0.5 %collective-permute-start.9 = (bf16[2,128,128]{2,1,0:T(8,128)(2,1)S(1)}, bf16[2,128,128]{2,1,0:T(8,128)(2,1)S(1)}, u32[]{:S(2)}, u32[]{:S(2)}) collective-permute-start(bf16[2,128,128]{2,1,0:T(8,128)(2,1)S(1)} %collective-permute-done.5.refs_2_), channel_id=1, source_target_pairs={{0,1},{1,0},{2,3},{3,2},{4,5},{5,4},{6,7},{7,6},{8,9},{9,8},{10,11... | collective-permute-start | bytes 196616 | tf_op jit(solution)/shard_map/ppermute | solution.py:206
  22.9 0.7 %collective-permute-done.6.refs_3_ = bf16[2,128,128]{2,1,0:T(8,128)(2,1)S(1)} collective-permute-done((bf16[2,128,128]{2,1,0:T(8,128)(2,1)S(1)}, bf16[2,128,128]{2,1,0:T(8,128)(2,1)S(1)}, u32[]{:S(2)}, u32[]{:S(2)}) %collective-permute-start.6) | collective-permute-done | bytes 65568 | tf_op jit(solution)/shard_map/ppermute | solution.py:206
  23.5 0.0 collective-permute-start.10
  23.5 0.4 %shard_map.112.refs_0_ = f32[8,8,128]{2,1,0:T(8,128)S(1)} custom-call(s32[1,128]{1,0:T(1,128)S(1)} %get-tuple-element.12.scalars, f32[8,128,128]{2,1,0:T(8,128)S(1)} %get-tuple-element.15.left_ref, bf16[2,128,128]{2,1,0:T(8,128)(2,1)S(1)} %broadcast_select_fusion.refs_0_, bf16[2,128,128]{2,1,0:T(8,128)(2,1)S(1)} %collective-permute-done.4.refs_1_, ...), custom_call_target="tpu_custom_call" | custom-call | tf_op jit(solution)/shard_map/pallas_call | solution.py:176
  23.9 0.0 collective-permute-done.7.refs_1_
  23.9 0.0 collective-permute-done.8.refs_2_
  23.9 0.0 collective-permute-done.9.refs_3_
  23.9 0.9 %collective-permute-done.10.refs_4_ = bf16[2,128,128]{2,1,0:T(8,128)(2,1)S(1)} collective-permute-done((bf16[2,128,128]{2,1,0:T(8,128)(2,1)S(1)}, bf16[2,128,128]{2,1,0:T(8,128)(2,1)S(1)}, u32[]{:S(2)}, u32[]{:S(2)}) %collective-permute-start.10) | collective-permute-done | bytes 65568 | tf_op jit(solution)/shard_map/ppermute | solution.py:206
  24.8 0.0 copy-done.3
  24.8 1.3 %shard_map.113 = bf16[8,16,128]{2,1,0:T(8,128)(2,1)} custom-call(s32[1,128]{1,0:T(1,128)S(1)} %get-tuple-element.12.scalars, f32[8,128,128]{2,1,0:T(8,128)S(1)} %get-tuple-element.15.left_ref, f32[8,16,128]{2,1,0:T(8,128)S(1)} %get-tuple-element.16.gate_ref, bf16[128,128]{1,0:T(8,128)(2,1)S(1)} %copy-done.3, f32[1,128]{1,0:T(1,128)S(1)} %get-tuple-element.17.gain_ref, ...), custom_call_target="tpu_custom_call" | custom-call | tf_op jit(solution)/shard_map/pallas_call | solution.py:176
  (1 shorter events, 0.0 us)
Async XLA Ops:
  0.0 6.9 %copy-start.7 = (f32[128]{0:T(128)S(1)}, f32[128]{0:T(128)}, u32[]{:S(2)}) copy-start(f32[128]{0:T(128)} %param.12) | copy-start | bytes 1540
  0.0 7.0 %copy-start.8 = (f32[128]{0:T(128)S(1)}, f32[128]{0:T(128)}, u32[]{:S(2)}) copy-start(f32[128]{0:T(128)} %param.19) | copy-start | bytes 1540
  0.0 10.8 %copy-start.1 = (bf16[128,128]{1,0:T(8,128)(2,1)S(1)}, bf16[128,128]{1,0:T(8,128)(2,1)}, u32[]{:S(2)}) copy-start(bf16[128,128]{1,0:T(8,128)(2,1)} %refs_5_.1) | copy-start | bytes 98308
  0.0 10.8 %copy-start.2 = (bf16[128,128]{1,0:T(8,128)(2,1)S(1)}, bf16[128,128]{1,0:T(8,128)(2,1)}, u32[]{:S(2)}) copy-start(bf16[128,128]{1,0:T(8,128)(2,1)} %refs_6_.1) | copy-start | bytes 98308
  1.0 12.9 %copy-start = (bf16[8,128,128]{2,1,0:T(8,128)(2,1)S(1)}, bf16[8,128,128]{2,1,0:T(8,128)(2,1)}, u32[]{:S(2)}) copy-start(bf16[8,128,128]{2,1,0:T(8,128)(2,1)} %x_ref.1) | copy-start | bytes 786436
  1.0 6.0 %collective-permute-start = (bf16[2,128,128]{2,1,0:T(8,128)(2,1)S(1)}, bf16[2,128,128]{2,1,0:T(8,128)(2,1)S(1)}, u32[]{:S(2)}, u32[]{:S(2)}) collective-permute-start(bf16[2,128,128]{2,1,0:T(8,128)(2,1)S(1)} %get-tuple-element.21), channel_id=1, source_target_pairs={{0,2},{1,3},{2,0},{3,1},{4,6},{5,7},{6,4},{7,5},{8,10},{9,11},{10,... | collective-permute-start | bytes 196616 | tf_op jit(solution)/shard_map/ppermute | solution.py:206
  4.1 4.8 %collective-permute-start.1 = (bf16[2,128,128]{2,1,0:T(8,128)(2,1)S(1)}, bf16[2,128,128]{2,1,0:T(8,128)(2,1)S(1)}, u32[]{:S(2)}, u32[]{:S(2)}) collective-permute-start(bf16[2,128,128]{2,1,0:T(8,128)(2,1)S(1)} %get-tuple-element.20), channel_id=1, source_target_pairs={{0,4},{1,5},{2,6},{3,7},{4,0},{5,1},{6,2},{7,3},{8,12},{9,13},{10,... | collective-permute-start | bytes 196616 | tf_op jit(solution)/shard_map/ppermute | solution.py:206
  5.6 5.2 %collective-permute-start.2 = (bf16[2,128,128]{2,1,0:T(8,128)(2,1)S(1)}, bf16[2,128,128]{2,1,0:T(8,128)(2,1)S(1)}, u32[]{:S(2)}, u32[]{:S(2)}) collective-permute-start(bf16[2,128,128]{2,1,0:T(8,128)(2,1)S(1)} %get-tuple-element.19), channel_id=1, source_target_pairs={{0,6},{1,7},{2,4},{3,5},{4,2},{5,3},{6,0},{7,1},{8,14},{9,15},{10,... | collective-permute-start | bytes 196616 | tf_op jit(solution)/shard_map/ppermute | solution.py:206
  10.8 3.1 %copy-start.4 = (bf16[128,128]{1,0:T(8,128)(2,1)S(1)}, bf16[128,128]{1,0:T(8,128)(2,1)}, u32[]{:S(2)}) copy-start(bf16[128,128]{1,0:T(8,128)(2,1)} %w_ref.1) | copy-start | bytes 98308
  10.8 3.1 %copy-start.5 = (bf16[128,128]{1,0:T(8,128)(2,1)S(1)}, bf16[128,128]{1,0:T(8,128)(2,1)}, u32[]{:S(2)}) copy-start(bf16[128,128]{1,0:T(8,128)(2,1)} %wg_ref.1) | copy-start | bytes 98308
  10.8 3.1 %copy-start.6 = (bf16[128,128]{1,0:T(8,128)(2,1)S(1)}, bf16[128,128]{1,0:T(8,128)(2,1)}, u32[]{:S(2)}) copy-start(bf16[128,128]{1,0:T(8,128)(2,1)} %wo_ref.1) | copy-start | bytes 98308
  11.3 5.8 %collective-permute-start.3 = (bf16[2,128,128]{2,1,0:T(8,128)(2,1)S(1)}, bf16[2,128,128]{2,1,0:T(8,128)(2,1)S(1)}, u32[]{:S(2)}, u32[]{:S(2)}) collective-permute-start(bf16[2,128,128]{2,1,0:T(8,128)(2,1)S(1)} %shard_map.110), channel_id=1, source_target_pairs={{0,8},{1,9},{2,10},{3,11},{4,12},{5,13},{6,14},{7,15},{8,0},{9,1},... | collective-permute-start | bytes 196616 | tf_op jit(solution)/shard_map/ppermute | solution.py:206
  17.1 7.7 %copy-start.3 = (bf16[128,128]{1,0:T(8,128)(2,1)S(1)}, bf16[128,128]{1,0:T(8,128)(2,1)}, u32[]{:S(2)}) copy-start(bf16[128,128]{1,0:T(8,128)(2,1)} %w_out_ref.1) | copy-start | bytes 98308
  17.1 5.2 %collective-permute-start.4 = (bf16[2,128,128]{2,1,0:T(8,128)(2,1)S(1)}, bf16[2,128,128]{2,1,0:T(8,128)(2,1)S(1)}, u32[]{:S(2)}, u32[]{:S(2)}) collective-permute-start(bf16[2,128,128]{2,1,0:T(8,128)(2,1)S(1)} %broadcast_select_fusion.refs_0_), channel_id=1, source_target_pairs={{0,6},{1,7},{2,4},{3,5},{4,2},{5,3},{6,0},{7,1},{8,14},{9,15},{10,... | collective-permute-start | bytes 196616 | tf_op jit(solution)/shard_map/ppermute | solution.py:206
  17.4 5.0 %collective-permute-start.5 = (bf16[2,128,128]{2,1,0:T(8,128)(2,1)S(1)}, bf16[2,128,128]{2,1,0:T(8,128)(2,1)S(1)}, u32[]{:S(2)}, u32[]{:S(2)}) collective-permute-start(bf16[2,128,128]{2,1,0:T(8,128)(2,1)S(1)} %broadcast_select_fusion.refs_0_), channel_id=1, source_target_pairs={{0,4},{1,5},{2,6},{3,7},{4,0},{5,1},{6,2},{7,3},{8,12},{9,13},{10,... | collective-permute-start | bytes 196616 | tf_op jit(solution)/shard_map/ppermute | solution.py:206
  19.3 4.3 %collective-permute-start.6 = (bf16[2,128,128]{2,1,0:T(8,128)(2,1)S(1)}, bf16[2,128,128]{2,1,0:T(8,128)(2,1)S(1)}, u32[]{:S(2)}, u32[]{:S(2)}) collective-permute-start(bf16[2,128,128]{2,1,0:T(8,128)(2,1)S(1)} %broadcast_select_fusion.refs_0_), channel_id=1, source_target_pairs={{0,2},{1,3},{2,0},{3,1},{4,6},{5,7},{6,4},{7,5},{8,10},{9,11},{10,... | collective-permute-start | bytes 196616 | tf_op jit(solution)/shard_map/ppermute | solution.py:206
  20.7 3.2 %collective-permute-start.7 = (bf16[2,128,128]{2,1,0:T(8,128)(2,1)S(1)}, bf16[2,128,128]{2,1,0:T(8,128)(2,1)S(1)}, u32[]{:S(2)}, u32[]{:S(2)}) collective-permute-start(bf16[2,128,128]{2,1,0:T(8,128)(2,1)S(1)} %broadcast_select_fusion.refs_0_), channel_id=1, source_target_pairs={{0,1},{1,0},{2,3},{3,2},{4,5},{5,4},{6,7},{7,6},{8,9},{9,8},{10,11... | collective-permute-start | bytes 196616 | tf_op jit(solution)/shard_map/ppermute | solution.py:206
  22.4 1.6 %collective-permute-start.8 = (bf16[2,128,128]{2,1,0:T(8,128)(2,1)S(1)}, bf16[2,128,128]{2,1,0:T(8,128)(2,1)S(1)}, u32[]{:S(2)}, u32[]{:S(2)}) collective-permute-start(bf16[2,128,128]{2,1,0:T(8,128)(2,1)S(1)} %collective-permute-done.4.refs_1_), channel_id=1, source_target_pairs={{0,1},{1,0},{2,3},{3,2},{4,5},{5,4},{6,7},{7,6},{8,9},{9,8},{10,11... | collective-permute-start | bytes 196616 | tf_op jit(solution)/shard_map/ppermute | solution.py:206
  22.4 1.6 %collective-permute-start.9 = (bf16[2,128,128]{2,1,0:T(8,128)(2,1)S(1)}, bf16[2,128,128]{2,1,0:T(8,128)(2,1)S(1)}, u32[]{:S(2)}, u32[]{:S(2)}) collective-permute-start(bf16[2,128,128]{2,1,0:T(8,128)(2,1)S(1)} %collective-permute-done.5.refs_2_), channel_id=1, source_target_pairs={{0,1},{1,0},{2,3},{3,2},{4,5},{5,4},{6,7},{7,6},{8,9},{9,8},{10,11... | collective-permute-start | bytes 196616 | tf_op jit(solution)/shard_map/ppermute | solution.py:206
  23.5 1.3 %collective-permute-start.10 = (bf16[2,128,128]{2,1,0:T(8,128)(2,1)S(1)}, bf16[2,128,128]{2,1,0:T(8,128)(2,1)S(1)}, u32[]{:S(2)}, u32[]{:S(2)}) collective-permute-start(bf16[2,128,128]{2,1,0:T(8,128)(2,1)S(1)} %collective-permute-done.6.refs_3_), channel_id=1, source_target_pairs={{0,1},{1,0},{2,3},{3,2},{4,5},{5,4},{6,7},{7,6},{8,9},{9,8},{10,11... | collective-permute-start | bytes 196616 | tf_op jit(solution)/shard_map/ppermute | solution.py:206

commit v3 on v2

--- a/solution.py
+++ b/solution.py
@@ -9,7 +9,9 @@
 
 BLOCKS = 8
 QUAD = 4
-GROUPS = ((0, 1, 2, 3), (4, 5, 6, 7))
+FIRST = (3, 2, 1)
+SECOND = (3, 1, 2)
+GROUPS = ((0, 1, 2, 3, 4, 5), (6, 7))
 VMEM = pl.BlockSpec(memory_space=pltpu.VMEM)
 
 
@@ -205,11 +207,11 @@
     def swap(values, mask):
         return lax.ppermute(values, "row", [(i, i ^ mask) for i in range(devices)])
 
-    got = {d: swap(pair_rows[d * small : (d + 1) * small], parts * d) for d in reversed(range(1, QUAD))}
+    got = {d: swap(pair_rows[d * small : (d + 1) * small], parts * d) for d in FIRST}
     right = local(
         functools.partial(right_body, chunk),
         jax.ShapeDtypeStruct((small, tokens, channels), bf16),
-        scalars, pair_rows[:small], *[got[d] for d in range(1, QUAD)], in_gain, w_right, w_right_gate,
+        scalars, pair_rows, *[got[d] for d in range(1, QUAD)], in_gain, w_right, w_right_gate,
     )
     left, gate = local(
         functools.partial(left_body, chunk),
@@ -226,7 +228,7 @@
         bit *= 2
 
     held, order = [right], [[(0, 0)]]
-    for d in reversed(range(1, QUAD)):
+    for d in SECOND:
         held.append(swap(right, parts * d))
         order.append([(0, d)])
     bit = 1

time: 26.3 us -> 25.5 us (0.970)
  waiting for transfers between devices: 9.4 us -> 7.95 us
  local copies, waits for them, and re-layouts: 1.03 us -> 1.65 us
    ppermute x11, waiting for transfers between devices: 9.4 us -> 7.95 us  [swap(): return lax.ppermute(values, 'row', [(i, i ^ mask) for i in range(devices)])]
    unnamed x18, local copies, waits for them, and re-layouts: 0.04 us -> 0.69 us
  transfers between devices with their start and end apart: 11 -> 11, of which waited for: 6 -> 5; matrix products, arithmetic and copies ran while one was open for 0% -> 0% of each run, Pallas kernels for 4% -> 5%
where the time goes in v3:
time: 25.5 us; the launch traced here: 25.3 us
  starting transfers between devices  11.4 us (45%)
  waiting for transfers between devices  7.95 us (31%)
  Pallas kernels  2.92 us (11%)
  local copies, waits for them, and re-layouts  1.65 us (6%)
  between operations  1.41 us (6%)
    ppermute x11, starting transfers between devices, swap(): return lax.ppermute(values, 'row', [(i, i ^ mask) for i in range(devices)])  11.4 us
    ppermute x11, waiting for transfers between devices, swap(): return lax.ppermute(values, 'row', [(i, i ^ mask) for i in range(devices)])  7.95 us
    pallas_call x4, Pallas kernels, local(): pl.pallas_call(body, out_shape=out_shape, in_specs=[VMEM] * (1 + len(oper...  2.84 us
    slice x1, local copies, waits for them, and re-layouts, on_device(): pair_rows[d * small:(d + 1) * small]  0.96 us
    unnamed x18, local copies, waits for them, and re-layouts  0.69 us
  transfers between devices with their start and end apart: 11, of which 5 were waited for; matrix products, arithmetic and copies ran while one was open for 0% of the time, Pallas kernels for 5%

profile of v3, /device:TPU:0, one launch (start us, length us, event | category | flops | bytes accessed | tf_op | source)
XLA Modules:
  0.0 25.3 jit_solution(4848146253161688101)
XLA Ops:
  0.0 0.0 copy-start
  0.0 0.0 copy-start.1
  0.0 0.0 copy-start.2
  0.0 1.0 %fusion = (bf16[2,128,128]{2,1,0:T(8,128)(2,1)S(1)}, bf16[2,128,128]{2,1,0:T(8,128)(2,1)S(1)}, bf16[2,128,128]{2,1,0:T(8,128)(2,1)S(1)}) fusion(bf16[8,128,128]{2,1,0:T(8,128)(2,1)} %x_ref.1), kind=kLoop, calls=%fused_computation.1 | loop fusion | bytes 393216 | tf_op jit(solution)/shard_map/slice | solution.py:210
  1.0 3.0 %collective-permute-start = (bf16[2,128,128]{2,1,0:T(8,128)(2,1)S(1)}, bf16[2,128,128]{2,1,0:T(8,128)(2,1)S(1)}, u32[]{:S(2)}, u32[]{:S(2)}) collective-permute-start(bf16[2,128,128]{2,1,0:T(8,128)(2,1)S(1)} %get-tuple-element.21), channel_id=1, source_target_pairs={{0,2},{1,3},{2,0},{3,1},{4,6},{5,7},{6,4},{7,5},{8,10},{9,11},{10,... | collective-permute-start | bytes 196616 | tf_op jit(solution)/shard_map/ppermute | solution.py:208
  4.0 1.6 %collective-permute-start.1 = (bf16[2,128,128]{2,1,0:T(8,128)(2,1)S(1)}, bf16[2,128,128]{2,1,0:T(8,128)(2,1)S(1)}, u32[]{:S(2)}, u32[]{:S(2)}) collective-permute-start(bf16[2,128,128]{2,1,0:T(8,128)(2,1)S(1)} %get-tuple-element.20), channel_id=1, source_target_pairs={{0,4},{1,5},{2,6},{3,7},{4,0},{5,1},{6,2},{7,3},{8,12},{9,13},{10,... | collective-permute-start | bytes 196616 | tf_op jit(solution)/shard_map/ppermute | solution.py:208
  5.6 0.0 collective-permute-start.2
  6.9 0.0 copy-start.7
  6.9 0.0 copy-start.8
  6.9 0.6 %copy-done.7 = f32[128]{0:T(128)S(1)} copy-done((f32[128]{0:T(128)S(1)}, f32[128]{0:T(128)}, u32[]{:S(2)}) %copy-start.7) | copy-done | bytes 536
  7.5 0.0 copy-done.8
  7.6 0.1 shard_map.109
  7.6 0.0 collective-permute-done.refs_1_
  7.6 1.1 %collective-permute-done.1.refs_2_ = bf16[2,128,128]{2,1,0:T(8,128)(2,1)S(1)} collective-permute-done((bf16[2,128,128]{2,1,0:T(8,128)(2,1)S(1)}, bf16[2,128,128]{2,1,0:T(8,128)(2,1)S(1)}, u32[]{:S(2)}, u32[]{:S(2)}) %collective-permute-start.1) | collective-permute-done | bytes 65568 | tf_op jit(solution)/shard_map/ppermute | solution.py:208
  8.8 1.9 %collective-permute-done.2.refs_3_ = bf16[2,128,128]{2,1,0:T(8,128)(2,1)S(1)} collective-permute-done((bf16[2,128,128]{2,1,0:T(8,128)(2,1)S(1)}, bf16[2,128,128]{2,1,0:T(8,128)(2,1)S(1)}, u32[]{:S(2)}, u32[]{:S(2)}) %collective-permute-start.2) | collective-permute-done | bytes 65568 | tf_op jit(solution)/shard_map/ppermute | solution.py:208
  10.7 0.0 copy-done
  10.7 0.0 copy-done.1
  10.8 0.0 copy-done.2
  10.8 0.0 copy-start.4
  10.8 0.0 copy-start.5
  10.8 0.0 copy-start.6
  10.8 0.5 %shard_map.110 = bf16[2,128,128]{2,1,0:T(8,128)(2,1)S(1)} custom-call(s32[1,128]{1,0:T(1,128)S(1)} %get-tuple-element.12.scalars, bf16[8,128,128]{2,1,0:T(8,128)(2,1)S(1)} %copy-done, bf16[2,128,128]{2,1,0:T(8,128)(2,1)S(1)} %collective-permute-done.refs_1_, bf16[2,128,128]{2,1,0:T(8,128)(2,1)S(1)} %collective-permute-done.1.refs_2_, ...), custom_call_target="tpu_custom_call" | custom-call | tf_op jit(solution)/shard_map/pallas_call | solution.py:178
  11.3 2.7 %collective-permute-start.3 = (bf16[2,128,128]{2,1,0:T(8,128)(2,1)S(1)}, bf16[2,128,128]{2,1,0:T(8,128)(2,1)S(1)}, u32[]{:S(2)}, u32[]{:S(2)}) collective-permute-start(bf16[2,128,128]{2,1,0:T(8,128)(2,1)S(1)} %shard_map.110), channel_id=1, source_target_pairs={{0,8},{1,9},{2,10},{3,11},{4,12},{5,13},{6,14},{7,15},{8,0},{9,1},... | collective-permute-start | bytes 196616 | tf_op jit(solution)/shard_map/ppermute | solution.py:208
  13.9 0.0 copy-done.4
  13.9 0.0 copy-done.5
  13.9 0.0 copy-done.6
  13.9 0.7 %shard_map.111 = (f32[8,128,128]{2,1,0:T(8,128)S(1)}, f32[8,16,128]{2,1,0:T(8,128)S(1)}) custom-call(s32[1,128]{1,0:T(1,128)S(1)} %get-tuple-element.12.scalars, bf16[8,128,128]{2,1,0:T(8,128)(2,1)S(1)} %copy-done, f32[1,128]{1,0:T(1,128)S(1)} %get-tuple-element.13.refs_4_.gain_ref, bf16[128,128]{1,0:T(8,128)(2,1)S(1)} %copy-done.4, ...), custom_call_target="tpu_custom_call" | custom-call | tf_op jit(solution)/shard_map/pallas_call | solution.py:178
  14.6 2.5 %collective-permute-done.3 = bf16[2,128,128]{2,1,0:T(8,128)(2,1)S(1)} collective-permute-done((bf16[2,128,128]{2,1,0:T(8,128)(2,1)S(1)}, bf16[2,128,128]{2,1,0:T(8,128)(2,1)S(1)}, u32[]{:S(2)}, u32[]{:S(2)}) %collective-permute-start.3) | collective-permute-done | bytes 65568 | tf_op jit(solution)/shard_map/ppermute | solution.py:208
  17.1 0.0 copy-start.3
  17.1 0.3 %collective-permute-start.4 = (bf16[2,128,128]{2,1,0:T(8,128)(2,1)S(1)}, bf16[2,128,128]{2,1,0:T(8,128)(2,1)S(1)}, u32[]{:S(2)}, u32[]{:S(2)}) collective-permute-start(bf16[2,128,128]{2,1,0:T(8,128)(2,1)S(1)} %broadcast_select_fusion.refs_0_), channel_id=1, source_target_pairs={{0,6},{1,7},{2,4},{3,5},{4,2},{5,3},{6,0},{7,1},{8,14},{9,15},{10,... | collective-permute-start | bytes 196616 | tf_op jit(solution)/shard_map/ppermute | solution.py:208
  17.4 1.2 %collective-permute-start.5 = (bf16[2,128,128]{2,1,0:T(8,128)(2,1)S(1)}, bf16[2,128,128]{2,1,0:T(8,128)(2,1)S(1)}, u32[]{:S(2)}, u32[]{:S(2)}) collective-permute-start(bf16[2,128,128]{2,1,0:T(8,128)(2,1)S(1)} %broadcast_select_fusion.refs_0_), channel_id=1, source_target_pairs={{0,2},{1,3},{2,0},{3,1},{4,6},{5,7},{6,4},{7,5},{8,10},{9,11},{10,... | collective-permute-start | bytes 196616 | tf_op jit(solution)/shard_map/ppermute | solution.py:208
  18.5 2.1 %collective-permute-start.6 = (bf16[2,128,128]{2,1,0:T(8,128)(2,1)S(1)}, bf16[2,128,128]{2,1,0:T(8,128)(2,1)S(1)}, u32[]{:S(2)}, u32[]{:S(2)}) collective-permute-start(bf16[2,128,128]{2,1,0:T(8,128)(2,1)S(1)} %broadcast_select_fusion.refs_0_), channel_id=1, source_target_pairs={{0,4},{1,5},{2,6},{3,7},{4,0},{5,1},{6,2},{7,3},{8,12},{9,13},{10,... | collective-permute-start | bytes 196616 | tf_op jit(solution)/shard_map/ppermute | solution.py:208
  20.7 0.0 collective-permute-start.7
  20.7 1.7 %collective-permute-done.4.refs_1_ = bf16[2,128,128]{2,1,0:T(8,128)(2,1)S(1)} collective-permute-done((bf16[2,128,128]{2,1,0:T(8,128)(2,1)S(1)}, bf16[2,128,128]{2,1,0:T(8,128)(2,1)S(1)}, u32[]{:S(2)}, u32[]{:S(2)}) %collective-permute-start.4) | collective-permute-done | bytes 65568 | tf_op jit(solution)/shard_map/ppermute | solution.py:208
  22.3 0.0 collective-permute-start.8
  22.3 0.0 collective-permute-done.5.refs_2_
  22.4 0.5 %collective-permute-start.9 = (bf16[2,128,128]{2,1,0:T(8,128)(2,1)S(1)}, bf16[2,128,128]{2,1,0:T(8,128)(2,1)S(1)}, u32[]{:S(2)}, u32[]{:S(2)}) collective-permute-start(bf16[2,128,128]{2,1,0:T(8,128)(2,1)S(1)} %collective-permute-done.5.refs_2_), channel_id=1, source_target_pairs={{0,1},{1,0},{2,3},{3,2},{4,5},{5,4},{6,7},{7,6},{8,9},{9,8},{10,11... | collective-permute-start | bytes 196616 | tf_op jit(solution)/shard_map/ppermute | solution.py:208
  22.9 0.0 collective-permute-done.6.refs_3_
  22.9 0.0 collective-permute-start.10
  22.9 0.0 collective-permute-done.7.refs_4_
  22.9 0.7 %collective-permute-done.8.refs_5_ = bf16[2,128,128]{2,1,0:T(8,128)(2,1)S(1)} collective-permute-done((bf16[2,128,128]{2,1,0:T(8,128)(2,1)S(1)}, bf16[2,128,128]{2,1,0:T(8,128)(2,1)S(1)}, u32[]{:S(2)}, u32[]{:S(2)}) %collective-permute-start.8) | collective-permute-done | bytes 65568 | tf_op jit(solution)/shard_map/ppermute | solution.py:208
  23.6 0.5 %shard_map.112.refs_0_ = f32[12,8,128]{2,1,0:T(8,128)S(1)} custom-call(s32[1,128]{1,0:T(1,128)S(1)} %get-tuple-element.12.scalars, f32[8,128,128]{2,1,0:T(8,128)S(1)} %get-tuple-element.15.left_ref, bf16[2,128,128]{2,1,0:T(8,128)(2,1)S(1)} %broadcast_select_fusion.refs_0_, bf16[2,128,128]{2,1,0:T(8,128)(2,1)S(1)} %collective-permute-done.4.refs_1_, ...), custom_call_target="tpu_custom_call" | custom-call | tf_op jit(solution)/shard_map/pallas_call | solution.py:178
  24.1 0.0 collective-permute-done.9.refs_1_
  24.2 0.0 collective-permute-done.10.refs_2_
  24.2 0.0 copy-done.3
  24.2 1.1 %shard_map.113 = bf16[8,16,128]{2,1,0:T(8,128)(2,1)} custom-call(s32[1,128]{1,0:T(1,128)S(1)} %get-tuple-element.12.scalars, f32[8,128,128]{2,1,0:T(8,128)S(1)} %get-tuple-element.15.left_ref, f32[8,16,128]{2,1,0:T(8,128)S(1)} %get-tuple-element.16.gate_ref, bf16[128,128]{1,0:T(8,128)(2,1)S(1)} %copy-done.3, f32[1,128]{1,0:T(1,128)S(1)} %get-tuple-element.17.gain_ref, ...), custom_call_target="tpu_custom_call" | custom-call | tf_op jit(solution)/shard_map/pallas_call | solution.py:178
  (1 shorter events, 0.0 us)
Async XLA Ops:
  0.0 10.7 %copy-start = (bf16[8,128,128]{2,1,0:T(8,128)(2,1)S(1)}, bf16[8,128,128]{2,1,0:T(8,128)(2,1)}, u32[]{:S(2)}) copy-start(bf16[8,128,128]{2,1,0:T(8,128)(2,1)} %x_ref.1) | copy-start | bytes 786436
  0.0 10.7 %copy-start.1 = (bf16[128,128]{1,0:T(8,128)(2,1)S(1)}, bf16[128,128]{1,0:T(8,128)(2,1)}, u32[]{:S(2)}) copy-start(bf16[128,128]{1,0:T(8,128)(2,1)} %refs_5_.1) | copy-start | bytes 98308
  0.0 10.7 %copy-start.2 = (bf16[128,128]{1,0:T(8,128)(2,1)S(1)}, bf16[128,128]{1,0:T(8,128)(2,1)}, u32[]{:S(2)}) copy-start(bf16[128,128]{1,0:T(8,128)(2,1)} %refs_6_.1) | copy-start | bytes 98308
  1.0 6.7 %collective-permute-start = (bf16[2,128,128]{2,1,0:T(8,128)(2,1)S(1)}, bf16[2,128,128]{2,1,0:T(8,128)(2,1)S(1)}, u32[]{:S(2)}, u32[]{:S(2)}) collective-permute-start(bf16[2,128,128]{2,1,0:T(8,128)(2,1)S(1)} %get-tuple-element.21), channel_id=1, source_target_pairs={{0,2},{1,3},{2,0},{3,1},{4,6},{5,7},{6,4},{7,5},{8,10},{9,11},{10,... | collective-permute-start | bytes 196616 | tf_op jit(solution)/shard_map/ppermute | solution.py:208
  4.0 4.8 %collective-permute-start.1 = (bf16[2,128,128]{2,1,0:T(8,128)(2,1)S(1)}, bf16[2,128,128]{2,1,0:T(8,128)(2,1)S(1)}, u32[]{:S(2)}, u32[]{:S(2)}) collective-permute-start(bf16[2,128,128]{2,1,0:T(8,128)(2,1)S(1)} %get-tuple-element.20), channel_id=1, source_target_pairs={{0,4},{1,5},{2,6},{3,7},{4,0},{5,1},{6,2},{7,3},{8,12},{9,13},{10,... | collective-permute-start | bytes 196616 | tf_op jit(solution)/shard_map/ppermute | solution.py:208
  5.6 5.2 %collective-permute-start.2 = (bf16[2,128,128]{2,1,0:T(8,128)(2,1)S(1)}, bf16[2,128,128]{2,1,0:T(8,128)(2,1)S(1)}, u32[]{:S(2)}, u32[]{:S(2)}) collective-permute-start(bf16[2,128,128]{2,1,0:T(8,128)(2,1)S(1)} %get-tuple-element.19), channel_id=1, source_target_pairs={{0,6},{1,7},{2,4},{3,5},{4,2},{5,3},{6,0},{7,1},{8,14},{9,15},{10,... | collective-permute-start | bytes 196616 | tf_op jit(solution)/shard_map/ppermute | solution.py:208
  6.9 0.7 %copy-start.7 = (f32[128]{0:T(128)S(1)}, f32[128]{0:T(128)}, u32[]{:S(2)}) copy-start(f32[128]{0:T(128)} %param.12) | copy-start | bytes 1540
  6.9 0.7 %copy-start.8 = (f32[128]{0:T(128)S(1)}, f32[128]{0:T(128)}, u32[]{:S(2)}) copy-start(f32[128]{0:T(128)} %param.19) | copy-start | bytes 1540
  10.8 3.2 %copy-start.4 = (bf16[128,128]{1,0:T(8,128)(2,1)S(1)}, bf16[128,128]{1,0:T(8,128)(2,1)}, u32[]{:S(2)}) copy-start(bf16[128,128]{1,0:T(8,128)(2,1)} %w_ref.1) | copy-start | bytes 98308
  10.8 3.1 %copy-start.5 = (bf16[128,128]{1,0:T(8,128)(2,1)S(1)}, bf16[128,128]{1,0:T(8,128)(2,1)}, u32[]{:S(2)}) copy-start(bf16[128,128]{1,0:T(8,128)(2,1)} %wg_ref.1) | copy-start | bytes 98308
  10.8 3.1 %copy-start.6 = (bf16[128,128]{1,0:T(8,128)(2,1)S(1)}, bf16[128,128]{1,0:T(8,128)(2,1)}, u32[]{:S(2)}) copy-start(bf16[128,128]{1,0:T(8,128)(2,1)} %wo_ref.1) | copy-start | bytes 98308
  11.3 5.8 %collective-permute-start.3 = (bf16[2,128,128]{2,1,0:T(8,128)(2,1)S(1)}, bf16[2,128,128]{2,1,0:T(8,128)(2,1)S(1)}, u32[]{:S(2)}, u32[]{:S(2)}) collective-permute-start(bf16[2,128,128]{2,1,0:T(8,128)(2,1)S(1)} %shard_map.110), channel_id=1, source_target_pairs={{0,8},{1,9},{2,10},{3,11},{4,12},{5,13},{6,14},{7,15},{8,0},{9,1},... | collective-permute-start | bytes 196616 | tf_op jit(solution)/shard_map/ppermute | solution.py:208
  17.1 7.1 %copy-start.3 = (bf16[128,128]{1,0:T(8,128)(2,1)S(1)}, bf16[128,128]{1,0:T(8,128)(2,1)}, u32[]{:S(2)}) copy-start(bf16[128,128]{1,0:T(8,128)(2,1)} %w_out_ref.1) | copy-start | bytes 98308
  17.1 5.2 %collective-permute-start.4 = (bf16[2,128,128]{2,1,0:T(8,128)(2,1)S(1)}, bf16[2,128,128]{2,1,0:T(8,128)(2,1)S(1)}, u32[]{:S(2)}, u32[]{:S(2)}) collective-permute-start(bf16[2,128,128]{2,1,0:T(8,128)(2,1)S(1)} %broadcast_select_fusion.refs_0_), channel_id=1, source_target_pairs={{0,6},{1,7},{2,4},{3,5},{4,2},{5,3},{6,0},{7,1},{8,14},{9,15},{10,... | collective-permute-start | bytes 196616 | tf_op jit(solution)/shard_map/ppermute | solution.py:208
  17.4 5.0 %collective-permute-start.5 = (bf16[2,128,128]{2,1,0:T(8,128)(2,1)S(1)}, bf16[2,128,128]{2,1,0:T(8,128)(2,1)S(1)}, u32[]{:S(2)}, u32[]{:S(2)}) collective-permute-start(bf16[2,128,128]{2,1,0:T(8,128)(2,1)S(1)} %broadcast_select_fusion.refs_0_), channel_id=1, source_target_pairs={{0,2},{1,3},{2,0},{3,1},{4,6},{5,7},{6,4},{7,5},{8,10},{9,11},{10,... | collective-permute-start | bytes 196616 | tf_op jit(solution)/shard_map/ppermute | solution.py:208
  18.5 4.3 %collective-permute-start.6 = (bf16[2,128,128]{2,1,0:T(8,128)(2,1)S(1)}, bf16[2,128,128]{2,1,0:T(8,128)(2,1)S(1)}, u32[]{:S(2)}, u32[]{:S(2)}) collective-permute-start(bf16[2,128,128]{2,1,0:T(8,128)(2,1)S(1)} %broadcast_select_fusion.refs_0_), channel_id=1, source_target_pairs={{0,4},{1,5},{2,6},{3,7},{4,0},{5,1},{6,2},{7,3},{8,12},{9,13},{10,... | collective-permute-start | bytes 196616 | tf_op jit(solution)/shard_map/ppermute | solution.py:208
  20.7 2.3 %collective-permute-start.7 = (bf16[2,128,128]{2,1,0:T(8,128)(2,1)S(1)}, bf16[2,128,128]{2,1,0:T(8,128)(2,1)S(1)}, u32[]{:S(2)}, u32[]{:S(2)}) collective-permute-start(bf16[2,128,128]{2,1,0:T(8,128)(2,1)S(1)} %broadcast_select_fusion.refs_0_), channel_id=1, source_target_pairs={{0,1},{1,0},{2,3},{3,2},{4,5},{5,4},{6,7},{7,6},{8,9},{9,8},{10,11... | collective-permute-start | bytes 196616 | tf_op jit(solution)/shard_map/ppermute | solution.py:208
  22.3 1.3 %collective-permute-start.8 = (bf16[2,128,128]{2,1,0:T(8,128)(2,1)S(1)}, bf16[2,128,128]{2,1,0:T(8,128)(2,1)S(1)}, u32[]{:S(2)}, u32[]{:S(2)}) collective-permute-start(bf16[2,128,128]{2,1,0:T(8,128)(2,1)S(1)} %collective-permute-done.4.refs_1_), channel_id=1, source_target_pairs={{0,1},{1,0},{2,3},{3,2},{4,5},{5,4},{6,7},{7,6},{8,9},{9,8},{10,11... | collective-permute-start | bytes 196616 | tf_op jit(solution)/shard_map/ppermute | solution.py:208
  22.4 1.8 %collective-permute-start.9 = (bf16[2,128,128]{2,1,0:T(8,128)(2,1)S(1)}, bf16[2,128,128]{2,1,0:T(8,128)(2,1)S(1)}, u32[]{:S(2)}, u32[]{:S(2)}) collective-permute-start(bf16[2,128,128]{2,1,0:T(8,128)(2,1)S(1)} %collective-permute-done.5.refs_2_), channel_id=1, source_target_pairs={{0,1},{1,0},{2,3},{3,2},{4,5},{5,4},{6,7},{7,6},{8,9},{9,8},{10,11... | collective-permute-start | bytes 196616 | tf_op jit(solution)/shard_map/ppermute | solution.py:208
  22.9 1.3 %collective-permute-start.10 = (bf16[2,128,128]{2,1,0:T(8,128)(2,1)S(1)}, bf16[2,128,128]{2,1,0:T(8,128)(2,1)S(1)}, u32[]{:S(2)}, u32[]{:S(2)}) collective-permute-start(bf16[2,128,128]{2,1,0:T(8,128)(2,1)S(1)} %collective-permute-done.6.refs_3_), channel_id=1, source_target_pairs={{0,1},{1,0},{2,3},{3,2},{4,5},{5,4},{6,7},{7,6},{8,9},{9,8},{10,11... | collective-permute-start | bytes 196616 | tf_op jit(solution)/shard_map/ppermute | solution.py:208

commit v4 on v3

--- a/solution.py
+++ b/solution.py
@@ -9,9 +9,10 @@
 
 BLOCKS = 8
 QUAD = 4
+CHUNK = 256
 FIRST = (3, 2, 1)
 SECOND = (3, 1, 2)
-GROUPS = ((0, 1, 2, 3, 4, 5), (6, 7))
+GROUPS = ((0, 1, 2, 3, 4), (5, 6, 7))
 VMEM = pl.BlockSpec(memory_space=pltpu.VMEM)
 
 
@@ -44,19 +45,24 @@
 
 
 def edge_rows(chunk, first, valid, read, gain_ref, w_ref, wg_ref, out_ref):
-    rows, tokens, _ = out_ref.shape
-    per_row = tokens // chunk
+    rows, tokens, channels = out_ref.shape
+    deep = min(tokens, chunk)
+    high = min(max(chunk // tokens, 1), rows)
+    per_row = tokens // deep
     gain = gain_ref[...]
-    ids = lax.broadcasted_iota(jnp.int32, (chunk, 1), 0)
+    joined = jnp.concatenate([wg_ref[...], w_ref[...]], axis=1)
+    ids = [lax.broadcasted_iota(jnp.int32, (high, deep, 1), axis) for axis in (0, 1)]
 
     def body(step):
-        row, col = step // per_row, (step % per_row) * chunk
-        here = jnp.logical_and(first + row < valid, ids + col < valid)
-        normed = layer_norm(read(row, pl.ds(col, chunk)).astype(jnp.float32), gain).astype(jnp.bfloat16)
-        edge = sigmoid(dot(normed, wg_ref[...])) * dot(normed, w_ref[...]) * here.astype(jnp.float32)
-        out_ref[row, pl.ds(col, chunk), :] = edge.astype(jnp.bfloat16).astype(out_ref.dtype)
-
-    steps(rows * per_row, body)
+        row, col = step // per_row * high, (step % per_row) * deep
+        here = jnp.logical_and(ids[0] + (first + row) < valid, ids[1] + col < valid)
+        values = read(pl.ds(row, high), pl.ds(col, deep)).astype(jnp.float32).reshape(high * deep, channels)
+        both = dot(layer_norm(values, gain).astype(jnp.bfloat16), joined)
+        edge = (sigmoid(both[:, :channels]) * both[:, channels:]).reshape(high, deep, channels)
+        edge = (edge * here.astype(jnp.float32)).astype(jnp.bfloat16)
+        out_ref[pl.ds(row, high), pl.ds(col, deep), :] = edge.astype(out_ref.dtype)
+
+    steps(rows // high * per_row, body)
 
 
 def left_body(chunk, scalars, x_ref, gain_ref, w_ref, wg_ref, wo_ref, out_ref, gate_ref):
@@ -76,12 +82,12 @@
 
 def right_body(chunk, scalars, *refs):
     candidates, (gain_ref, w_ref, wg_ref, out_ref) = refs[:-4], refs[-4:]
-    which = scalar(scalars, 4)
+    which = scalars[0:1, 4:5].reshape(1, 1, 1)
 
     def read(row, at):
-        value = candidates[0][row, at, :]
+        value = candidates[0][row, at, :].astype(jnp.float32)
         for d in range(1, len(candidates)):
-            value = jnp.where(which == d, candidates[d][row, at, :], value)
+            value = jnp.where(which == d, candidates[d][row, at, :].astype(jnp.float32), value)
         return value
 
     edge_rows(chunk, scalar(scalars, 3), scalar(scalars, 0), read, gain_ref, w_ref, wg_ref, out_ref)
@@ -116,16 +122,22 @@
             store(base + t, at_piece * small + t, total)
 
 
-def early_body(order, small, scalars, left_ref, *refs):
-    right_refs, out_ref, lanes = refs[:-2], refs[-2], refs[-1]
+def project(product, w_out_ref, gain_ref):
+    normed = layer_norm(product, gain_ref[...]).astype(jnp.bfloat16)
+    return dot(normed, w_out_ref[...])
+
+
+def early_body(order, small, scalars, left_ref, w_out_ref, gain_ref, *refs):
+    right_refs, out_ref, product, lanes = refs[:-3], refs[-3], refs[-2], refs[-1]
     at_row = 0
     for right_ref, places in zip(right_refs, order):
 
         def store(j, held_at, total, at_row=at_row):
-            out_ref[at_row + held_at] = total
+            product[at_row + held_at] = total
 
         contract(places, small, scalar(scalars, 4), scalar(scalars, 5), left_ref, right_ref, lanes, store)
         at_row += right_ref.shape[0]
+    out_ref[...] = project(product[...].reshape(-1, product.shape[-1]), w_out_ref, gain_ref).reshape(out_ref.shape)
 
 
 def finish_body(early_order, n_early, order, small, scalars, left_ref, gate_ref, w_out_ref, gain_ref, *refs):
@@ -133,20 +145,28 @@
     rows, tokens, channels = left_ref.shape
     width = out_ref.shape[1]
     which, part = scalar(scalars, 4), scalar(scalars, 5)
-    right_refs = refs[:-4]
-    early_rows = [ref.at[t] for ref in right_refs[:n_early] for t in range(ref.shape[0])]
-    right_refs = right_refs[n_early:]
-    for at_piece, (p, d) in enumerate(sum(early_order, [])):
+    early_refs, right_refs = refs[:n_early], refs[n_early:-4]
+
+    def row_of(place, t):
+        return ((part ^ place[0]) * rows + (which ^ place[1]) * small + t) * rows
+
+    at_row = 0
+    for right_ref, places in zip(right_refs, order):
+
+        def store(j, held_at, total, at_row=at_row):
+            product[at_row + held_at] = total
+
+        contract(places, small, which, part, left_ref, right_ref, lanes, store)
+        at_row += right_ref.shape[0]
+    late = project(product[...].reshape(-1, channels), w_out_ref, gain_ref)
+    for at_piece, place in enumerate(sum(order, [])):
         for t in range(small):
-            product[(part ^ p) * rows + (which ^ d) * small + t] = early_rows[at_piece * small + t][...]
-
-    def store(j, held_at, total):
-        product[j] = total
-
-    for right_ref, places in zip(right_refs, order):
-        contract(places, small, which, part, left_ref, right_ref, lanes, store)
-    normed = layer_norm(product[...].reshape(width * rows, channels), gain_ref[...]).astype(jnp.bfloat16)
-    result[...] = dot(normed, w_out_ref[...])
+            at = (at_piece * small + t) * rows
+            result[pl.ds(row_of(place, t), rows), :] = late[at : at + rows]
+    early_rows = [ref.at[t] for ref in early_refs for t in range(ref.shape[0])]
+    for at_piece, place in enumerate(sum(early_order, [])):
+        for t in range(small):
+            result[pl.ds(row_of(place, t), rows), :] = early_rows[at_piece * small + t][...]
     for i in range(rows):
         out_ref[i] = (gate_ref[i] * result[pl.ds(i, width, stride=rows), :]).astype(jnp.bfloat16)
 
@@ -192,7 +212,7 @@
     width = tokens // BLOCKS
     parts = width // rows
     small = rows // QUAD
-    chunk = min(tokens, 128)
+    chunk = CHUNK
     bf16, f32 = jnp.bfloat16, jnp.float32
     differs = lax.div(lax.axis_index("row").astype(jnp.int32), parts) ^ window[0]
     gain_shape = jax.ShapeDtypeStruct((1, channels), f32)
@@ -239,7 +259,7 @@
         order = order + [[(p ^ bit, d) for p, d in places] for places in order]
         bit *= 2
 
-    lanes = pltpu.VMEM((small * rows * 8, channels), f32)
+    lanes = pltpu.VMEM(((small * rows + 1) * 8, channels), f32)
     groups = GROUPS if len(held) == 8 else (range(len(held)),)
     early, early_order = [], []
     for group in groups[:-1]:
@@ -249,8 +269,8 @@
             local(
                 functools.partial(early_body, chosen, small),
                 jax.ShapeDtypeStruct((sum(held[i].shape[0] for i in group), rows, channels), f32),
-                scalars, left, *[held[i] for i in group],
-                scratch=[lanes],
+                scalars, left, w_out, out_gain, *[held[i] for i in group],
+                scratch=[pltpu.VMEM((sum(held[i].shape[0] for i in group), rows, channels), f32), lanes],
             )
         )
     late_order = [order[i] for i in groups[-1]]
@@ -259,7 +279,11 @@
         functools.partial(finish_body, early_order, len(early), late_order, small),
         jax.ShapeDtypeStruct((rows, width, channels), bf16),
         scalars, left, gate, w_out, out_gain, *early, *late,
-        scratch=[pltpu.VMEM((width, rows, channels), f32), pltpu.VMEM((width * rows, channels), f32), lanes],
+        scratch=[
+            pltpu.VMEM((sum(h.shape[0] for h in late), rows, channels), f32),
+            pltpu.VMEM(((width + 1) * rows, channels), f32),
+            lanes,
+        ],
     )
 
 

time: 25.5 us -> 25.5 us (level)
  transfers between devices with their start and end apart: 11 -> 11, of which waited for: 5 -> 6; matrix products, arithmetic and copies ran while one was open for 0% -> 0% of each run, Pallas kernels for 5% -> 6%
where the time goes in v4:
time: 25.5 us; the launch traced here: 25.3 us
  starting transfers between devices  11.4 us (45%)
  waiting for transfers between devices  7.8 us (31%)
  Pallas kernels  3.08 us (12%)
  local copies, waits for them, and re-layouts  1.65 us (6%)
  between operations  1.38 us (5%)
    ppermute x11, starting transfers between devices, swap(): return lax.ppermute(values, 'row', [(i, i ^ mask) for i in range(devices)])  11.4 us
    ppermute x11, waiting for transfers between devices, swap(): return lax.ppermute(values, 'row', [(i, i ^ mask) for i in range(devices)])  7.8 us
    pallas_call x4, Pallas kernels, local(): pl.pallas_call(body, out_shape=out_shape, in_specs=[VMEM] * (1 + len(oper...  2.99 us
    slice x1, local copies, waits for them, and re-layouts, on_device(): pair_rows[d * small:(d + 1) * small]  0.96 us
    unnamed x18, local copies, waits for them, and re-layouts  0.69 us
  transfers between devices with their start and end apart: 11, of which 6 were waited for; matrix products, arithmetic and copies ran while one was open for 0% of the time, Pallas kernels for 6%

profile of v4, /device:TPU:0, one launch (start us, length us, event | category | flops | bytes accessed | tf_op | source)
XLA Modules:
  0.0 25.3 jit_solution(12372518655859014149)
XLA Ops:
  0.0 0.0 copy-start
  0.0 0.0 copy-start.2
  0.0 0.0 copy-start.3
  0.0 1.0 %fusion = (bf16[2,128,128]{2,1,0:T(8,128)(2,1)S(1)}, bf16[2,128,128]{2,1,0:T(8,128)(2,1)S(1)}, bf16[2,128,128]{2,1,0:T(8,128)(2,1)S(1)}) fusion(bf16[8,128,128]{2,1,0:T(8,128)(2,1)} %x_ref.1), kind=kLoop, calls=%fused_computation.1 | loop fusion | bytes 393216 | tf_op jit(solution)/shard_map/slice | solution.py:230
  1.0 3.0 %collective-permute-start = (bf16[2,128,128]{2,1,0:T(8,128)(2,1)S(1)}, bf16[2,128,128]{2,1,0:T(8,128)(2,1)S(1)}, u32[]{:S(2)}, u32[]{:S(2)}) collective-permute-start(bf16[2,128,128]{2,1,0:T(8,128)(2,1)S(1)} %get-tuple-element.21), channel_id=1, source_target_pairs={{0,2},{1,3},{2,0},{3,1},{4,6},{5,7},{6,4},{7,5},{8,10},{9,11},{10,... | collective-permute-start | bytes 196616 | tf_op jit(solution)/shard_map/ppermute | solution.py:228
  4.0 1.6 %collective-permute-start.1 = (bf16[2,128,128]{2,1,0:T(8,128)(2,1)S(1)}, bf16[2,128,128]{2,1,0:T(8,128)(2,1)S(1)}, u32[]{:S(2)}, u32[]{:S(2)}) collective-permute-start(bf16[2,128,128]{2,1,0:T(8,128)(2,1)S(1)} %get-tuple-element.20), channel_id=1, source_target_pairs={{0,4},{1,5},{2,6},{3,7},{4,0},{5,1},{6,2},{7,3},{8,12},{9,13},{10,... | collective-permute-start | bytes 196616 | tf_op jit(solution)/shard_map/ppermute | solution.py:228
  5.6 0.0 collective-permute-start.2
  6.9 0.0 copy-start.7
  6.9 0.0 copy-start.8
  6.9 0.6 %copy-done.7 = f32[128]{0:T(128)S(1)} copy-done((f32[128]{0:T(128)S(1)}, f32[128]{0:T(128)}, u32[]{:S(2)}) %copy-start.7) | copy-done | bytes 536
  7.5 0.0 copy-done.8
  7.6 0.1 shard_map.109
  7.6 0.0 collective-permute-done.refs_1_
  7.6 1.1 %collective-permute-done.1.refs_2_ = bf16[2,128,128]{2,1,0:T(8,128)(2,1)S(1)} collective-permute-done((bf16[2,128,128]{2,1,0:T(8,128)(2,1)S(1)}, bf16[2,128,128]{2,1,0:T(8,128)(2,1)S(1)}, u32[]{:S(2)}, u32[]{:S(2)}) %collective-permute-start.1) | collective-permute-done | bytes 65568 | tf_op jit(solution)/shard_map/ppermute | solution.py:228
  8.8 1.9 %collective-permute-done.2.refs_3_ = bf16[2,128,128]{2,1,0:T(8,128)(2,1)S(1)} collective-permute-done((bf16[2,128,128]{2,1,0:T(8,128)(2,1)S(1)}, bf16[2,128,128]{2,1,0:T(8,128)(2,1)S(1)}, u32[]{:S(2)}, u32[]{:S(2)}) %collective-permute-start.2) | collective-permute-done | bytes 65568 | tf_op jit(solution)/shard_map/ppermute | solution.py:228
  10.7 0.0 copy-done
  10.7 0.0 copy-done.2
  10.8 0.0 copy-done.3
  10.8 0.0 copy-start.4
  10.8 0.0 copy-start.5
  10.8 0.0 copy-start.6
  10.8 0.4 %shard_map.110 = bf16[2,128,128]{2,1,0:T(8,128)(2,1)S(1)} custom-call(s32[1,128]{1,0:T(1,128)S(1)} %get-tuple-element.12.scalars, bf16[8,128,128]{2,1,0:T(8,128)(2,1)S(1)} %copy-done, bf16[2,128,128]{2,1,0:T(8,128)(2,1)S(1)} %collective-permute-done.refs_1_, bf16[2,128,128]{2,1,0:T(8,128)(2,1)S(1)} %collective-permute-done.1.refs_2_, ...), custom_call_target="tpu_custom_call" | custom-call | tf_op jit(solution)/shard_map/pallas_call | solution.py:198
  11.2 2.7 %collective-permute-start.3 = (bf16[2,128,128]{2,1,0:T(8,128)(2,1)S(1)}, bf16[2,128,128]{2,1,0:T(8,128)(2,1)S(1)}, u32[]{:S(2)}, u32[]{:S(2)}) collective-permute-start(bf16[2,128,128]{2,1,0:T(8,128)(2,1)S(1)} %shard_map.110), channel_id=1, source_target_pairs={{0,8},{1,9},{2,10},{3,11},{4,12},{5,13},{6,14},{7,15},{8,0},{9,1},... | collective-permute-start | bytes 196616 | tf_op jit(solution)/shard_map/ppermute | solution.py:228
  13.9 0.0 copy-done.4
  13.9 0.0 copy-done.5
  13.9 0.0 copy-done.6
  13.9 0.7 %shard_map.111 = (f32[8,128,128]{2,1,0:T(8,128)S(1)}, f32[8,16,128]{2,1,0:T(8,128)S(1)}) custom-call(s32[1,128]{1,0:T(1,128)S(1)} %get-tuple-element.12.scalars, bf16[8,128,128]{2,1,0:T(8,128)(2,1)S(1)} %copy-done, f32[1,128]{1,0:T(1,128)S(1)} %get-tuple-element.13.refs_4_.gain_ref, bf16[128,128]{1,0:T(8,128)(2,1)S(1)} %copy-done.4, ...), custom_call_target="tpu_custom_call" | custom-call | tf_op jit(solution)/shard_map/pallas_call | solution.py:198
  14.6 2.5 %collective-permute-done.3 = bf16[2,128,128]{2,1,0:T(8,128)(2,1)S(1)} collective-permute-done((bf16[2,128,128]{2,1,0:T(8,128)(2,1)S(1)}, bf16[2,128,128]{2,1,0:T(8,128)(2,1)S(1)}, u32[]{:S(2)}, u32[]{:S(2)}) %collective-permute-start.3) | collective-permute-done | bytes 65568 | tf_op jit(solution)/shard_map/ppermute | solution.py:228
  17.0 0.0 copy-start.1
  17.0 0.3 %collective-permute-start.4 = (bf16[2,128,128]{2,1,0:T(8,128)(2,1)S(1)}, bf16[2,128,128]{2,1,0:T(8,128)(2,1)S(1)}, u32[]{:S(2)}, u32[]{:S(2)}) collective-permute-start(bf16[2,128,128]{2,1,0:T(8,128)(2,1)S(1)} %broadcast_select_fusion.refs_0_), channel_id=1, source_target_pairs={{0,6},{1,7},{2,4},{3,5},{4,2},{5,3},{6,0},{7,1},{8,14},{9,15},{10,... | collective-permute-start | bytes 196616 | tf_op jit(solution)/shard_map/ppermute | solution.py:228
  17.3 1.2 %collective-permute-start.5 = (bf16[2,128,128]{2,1,0:T(8,128)(2,1)S(1)}, bf16[2,128,128]{2,1,0:T(8,128)(2,1)S(1)}, u32[]{:S(2)}, u32[]{:S(2)}) collective-permute-start(bf16[2,128,128]{2,1,0:T(8,128)(2,1)S(1)} %broadcast_select_fusion.refs_0_), channel_id=1, source_target_pairs={{0,2},{1,3},{2,0},{3,1},{4,6},{5,7},{6,4},{7,5},{8,10},{9,11},{10,... | collective-permute-start | bytes 196616 | tf_op jit(solution)/shard_map/ppermute | solution.py:228
  18.5 2.1 %collective-permute-start.6 = (bf16[2,128,128]{2,1,0:T(8,128)(2,1)S(1)}, bf16[2,128,128]{2,1,0:T(8,128)(2,1)S(1)}, u32[]{:S(2)}, u32[]{:S(2)}) collective-permute-start(bf16[2,128,128]{2,1,0:T(8,128)(2,1)S(1)} %broadcast_select_fusion.refs_0_), channel_id=1, source_target_pairs={{0,4},{1,5},{2,6},{3,7},{4,0},{5,1},{6,2},{7,3},{8,12},{9,13},{10,... | collective-permute-start | bytes 196616 | tf_op jit(solution)/shard_map/ppermute | solution.py:228
  20.6 0.0 collective-permute-start.7
  20.6 1.7 %collective-permute-done.4.refs_1_ = bf16[2,128,128]{2,1,0:T(8,128)(2,1)S(1)} collective-permute-done((bf16[2,128,128]{2,1,0:T(8,128)(2,1)S(1)}, bf16[2,128,128]{2,1,0:T(8,128)(2,1)S(1)}, u32[]{:S(2)}, u32[]{:S(2)}) %collective-permute-start.4) | collective-permute-done | bytes 65568 | tf_op jit(solution)/shard_map/ppermute | solution.py:228
  22.3 0.0 collective-permute-start.8
  22.3 0.0 collective-permute-done.5.refs_2_
  22.3 0.5 %collective-permute-start.9 = (bf16[2,128,128]{2,1,0:T(8,128)(2,1)S(1)}, bf16[2,128,128]{2,1,0:T(8,128)(2,1)S(1)}, u32[]{:S(2)}, u32[]{:S(2)}) collective-permute-start(bf16[2,128,128]{2,1,0:T(8,128)(2,1)S(1)} %collective-permute-done.5.refs_2_), channel_id=1, source_target_pairs={{0,1},{1,0},{2,3},{3,2},{4,5},{5,4},{6,7},{7,6},{8,9},{9,8},{10,11... | collective-permute-start | bytes 196616 | tf_op jit(solution)/shard_map/ppermute | solution.py:228
  22.8 0.0 collective-permute-done.6.refs_3_
  22.8 0.0 collective-permute-start.10
  22.9 0.0 collective-permute-done.7.refs_4_
  22.9 0.0 copy-done.1
  22.9 0.7 %shard_map.112.refs_0_ = f32[10,8,128]{2,1,0:T(8,128)S(1)} custom-call(s32[1,128]{1,0:T(1,128)S(1)} %get-tuple-element.12.scalars, f32[8,128,128]{2,1,0:T(8,128)S(1)} %get-tuple-element.15.left_ref, bf16[128,128]{1,0:T(8,128)(2,1)S(1)} %copy-done.1, f32[1,128]{1,0:T(1,128)S(1)} %get-tuple-element.17.gain_ref, ...), custom_call_target="tpu_custom_call" | custom-call | tf_op jit(solution)/shard_map/pallas_call | solution.py:198
  23.6 0.0 collective-permute-done.8.refs_1_
  23.6 0.1 collective-permute-done.9.refs_2_
  23.7 0.4 %collective-permute-done.10.refs_3_ = bf16[2,128,128]{2,1,0:T(8,128)(2,1)S(1)} collective-permute-done((bf16[2,128,128]{2,1,0:T(8,128)(2,1)S(1)}, bf16[2,128,128]{2,1,0:T(8,128)(2,1)S(1)}, u32[]{:S(2)}, u32[]{:S(2)}) %collective-permute-start.10) | collective-permute-done | bytes 65568 | tf_op jit(solution)/shard_map/ppermute | solution.py:228
  24.1 1.2 %shard_map.113 = bf16[8,16,128]{2,1,0:T(8,128)(2,1)} custom-call(s32[1,128]{1,0:T(1,128)S(1)} %get-tuple-element.12.scalars, f32[8,128,128]{2,1,0:T(8,128)S(1)} %get-tuple-element.15.left_ref, f32[8,16,128]{2,1,0:T(8,128)S(1)} %get-tuple-element.16.gate_ref, bf16[128,128]{1,0:T(8,128)(2,1)S(1)} %copy-done.1, f32[1,128]{1,0:T(1,128)S(1)} %get-tuple-element.17.gain_ref, ...), custom_call_target="tpu_custom_call" | custom-call | tf_op jit(solution)/shard_map/pallas_call | solution.py:198
  (1 shorter events, 0.0 us)
Async XLA Ops:
  0.0 10.7 %copy-start = (bf16[8,128,128]{2,1,0:T(8,128)(2,1)S(1)}, bf16[8,128,128]{2,1,0:T(8,128)(2,1)}, u32[]{:S(2)}) copy-start(bf16[8,128,128]{2,1,0:T(8,128)(2,1)} %x_ref.1) | copy-start | bytes 786436
  0.0 10.7 %copy-start.2 = (bf16[128,128]{1,0:T(8,128)(2,1)S(1)}, bf16[128,128]{1,0:T(8,128)(2,1)}, u32[]{:S(2)}) copy-start(bf16[128,128]{1,0:T(8,128)(2,1)} %refs_5_.1) | copy-start | bytes 98308
  0.0 10.7 %copy-start.3 = (bf16[128,128]{1,0:T(8,128)(2,1)S(1)}, bf16[128,128]{1,0:T(8,128)(2,1)}, u32[]{:S(2)}) copy-start(bf16[128,128]{1,0:T(8,128)(2,1)} %refs_6_.1) | copy-start | bytes 98308
  1.0 6.7 %collective-permute-start = (bf16[2,128,128]{2,1,0:T(8,128)(2,1)S(1)}, bf16[2,128,128]{2,1,0:T(8,128)(2,1)S(1)}, u32[]{:S(2)}, u32[]{:S(2)}) collective-permute-start(bf16[2,128,128]{2,1,0:T(8,128)(2,1)S(1)} %get-tuple-element.21), channel_id=1, source_target_pairs={{0,2},{1,3},{2,0},{3,1},{4,6},{5,7},{6,4},{7,5},{8,10},{9,11},{10,... | collective-permute-start | bytes 196616 | tf_op jit(solution)/shard_map/ppermute | solution.py:228
  4.0 4.8 %collective-permute-start.1 = (bf16[2,128,128]{2,1,0:T(8,128)(2,1)S(1)}, bf16[2,128,128]{2,1,0:T(8,128)(2,1)S(1)}, u32[]{:S(2)}, u32[]{:S(2)}) collective-permute-start(bf16[2,128,128]{2,1,0:T(8,128)(2,1)S(1)} %get-tuple-element.20), channel_id=1, source_target_pairs={{0,4},{1,5},{2,6},{3,7},{4,0},{5,1},{6,2},{7,3},{8,12},{9,13},{10,... | collective-permute-start | bytes 196616 | tf_op jit(solution)/shard_map/ppermute | solution.py:228
  5.6 5.2 %collective-permute-start.2 = (bf16[2,128,128]{2,1,0:T(8,128)(2,1)S(1)}, bf16[2,128,128]{2,1,0:T(8,128)(2,1)S(1)}, u32[]{:S(2)}, u32[]{:S(2)}) collective-permute-start(bf16[2,128,128]{2,1,0:T(8,128)(2,1)S(1)} %get-tuple-element.19), channel_id=1, source_target_pairs={{0,6},{1,7},{2,4},{3,5},{4,2},{5,3},{6,0},{7,1},{8,14},{9,15},{10,... | collective-permute-start | bytes 196616 | tf_op jit(solution)/shard_map/ppermute | solution.py:228
  6.9 0.7 %copy-start.7 = (f32[128]{0:T(128)S(1)}, f32[128]{0:T(128)}, u32[]{:S(2)}) copy-start(f32[128]{0:T(128)} %param.12) | copy-start | bytes 1540
  6.9 0.7 %copy-start.8 = (f32[128]{0:T(128)S(1)}, f32[128]{0:T(128)}, u32[]{:S(2)}) copy-start(f32[128]{0:T(128)} %param.19) | copy-start | bytes 1540
  10.8 3.1 %copy-start.4 = (bf16[128,128]{1,0:T(8,128)(2,1)S(1)}, bf16[128,128]{1,0:T(8,128)(2,1)}, u32[]{:S(2)}) copy-start(bf16[128,128]{1,0:T(8,128)(2,1)} %w_ref.1) | copy-start | bytes 98308
  10.8 3.1 %copy-start.5 = (bf16[128,128]{1,0:T(8,128)(2,1)S(1)}, bf16[128,128]{1,0:T(8,128)(2,1)}, u32[]{:S(2)}) copy-start(bf16[128,128]{1,0:T(8,128)(2,1)} %wg_ref.1) | copy-start | bytes 98308
  10.8 3.1 %copy-start.6 = (bf16[128,128]{1,0:T(8,128)(2,1)S(1)}, bf16[128,128]{1,0:T(8,128)(2,1)}, u32[]{:S(2)}) copy-start(bf16[128,128]{1,0:T(8,128)(2,1)} %wo_ref.1) | copy-start | bytes 98308
  11.2 5.8 %collective-permute-start.3 = (bf16[2,128,128]{2,1,0:T(8,128)(2,1)S(1)}, bf16[2,128,128]{2,1,0:T(8,128)(2,1)S(1)}, u32[]{:S(2)}, u32[]{:S(2)}) collective-permute-start(bf16[2,128,128]{2,1,0:T(8,128)(2,1)S(1)} %shard_map.110), channel_id=1, source_target_pairs={{0,8},{1,9},{2,10},{3,11},{4,12},{5,13},{6,14},{7,15},{8,0},{9,1},... | collective-permute-start | bytes 196616 | tf_op jit(solution)/shard_map/ppermute | solution.py:228
  17.0 5.9 %copy-start.1 = (bf16[128,128]{1,0:T(8,128)(2,1)S(1)}, bf16[128,128]{1,0:T(8,128)(2,1)}, u32[]{:S(2)}) copy-start(bf16[128,128]{1,0:T(8,128)(2,1)} %w_out_ref.3) | copy-start | bytes 98308
  17.0 5.2 %collective-permute-start.4 = (bf16[2,128,128]{2,1,0:T(8,128)(2,1)S(1)}, bf16[2,128,128]{2,1,0:T(8,128)(2,1)S(1)}, u32[]{:S(2)}, u32[]{:S(2)}) collective-permute-start(bf16[2,128,128]{2,1,0:T(8,128)(2,1)S(1)} %broadcast_select_fusion.refs_0_), channel_id=1, source_target_pairs={{0,6},{1,7},{2,4},{3,5},{4,2},{5,3},{6,0},{7,1},{8,14},{9,15},{10,... | collective-permute-start | bytes 196616 | tf_op jit(solution)/shard_map/ppermute | solution.py:228
  17.3 5.0 %collective-permute-start.5 = (bf16[2,128,128]{2,1,0:T(8,128)(2,1)S(1)}, bf16[2,128,128]{2,1,0:T(8,128)(2,1)S(1)}, u32[]{:S(2)}, u32[]{:S(2)}) collective-permute-start(bf16[2,128,128]{2,1,0:T(8,128)(2,1)S(1)} %broadcast_select_fusion.refs_0_), channel_id=1, source_target_pairs={{0,2},{1,3},{2,0},{3,1},{4,6},{5,7},{6,4},{7,5},{8,10},{9,11},{10,... | collective-permute-start | bytes 196616 | tf_op jit(solution)/shard_map/ppermute | solution.py:228
  18.5 4.3 %collective-permute-start.6 = (bf16[2,128,128]{2,1,0:T(8,128)(2,1)S(1)}, bf16[2,128,128]{2,1,0:T(8,128)(2,1)S(1)}, u32[]{:S(2)}, u32[]{:S(2)}) collective-permute-start(bf16[2,128,128]{2,1,0:T(8,128)(2,1)S(1)} %broadcast_select_fusion.refs_0_), channel_id=1, source_target_pairs={{0,4},{1,5},{2,6},{3,7},{4,0},{5,1},{6,2},{7,3},{8,12},{9,13},{10,... | collective-permute-start | bytes 196616 | tf_op jit(solution)/shard_map/ppermute | solution.py:228
  20.6 2.3 %collective-permute-start.7 = (bf16[2,128,128]{2,1,0:T(8,128)(2,1)S(1)}, bf16[2,128,128]{2,1,0:T(8,128)(2,1)S(1)}, u32[]{:S(2)}, u32[]{:S(2)}) collective-permute-start(bf16[2,128,128]{2,1,0:T(8,128)(2,1)S(1)} %broadcast_select_fusion.refs_0_), channel_id=1, source_target_pairs={{0,1},{1,0},{2,3},{3,2},{4,5},{5,4},{6,7},{7,6},{8,9},{9,8},{10,11... | collective-permute-start | bytes 196616 | tf_op jit(solution)/shard_map/ppermute | solution.py:228
  22.3 1.3 %collective-permute-start.8 = (bf16[2,128,128]{2,1,0:T(8,128)(2,1)S(1)}, bf16[2,128,128]{2,1,0:T(8,128)(2,1)S(1)}, u32[]{:S(2)}, u32[]{:S(2)}) collective-permute-start(bf16[2,128,128]{2,1,0:T(8,128)(2,1)S(1)} %collective-permute-done.4.refs_1_), channel_id=1, source_target_pairs={{0,1},{1,0},{2,3},{3,2},{4,5},{5,4},{6,7},{7,6},{8,9},{9,8},{10,11... | collective-permute-start | bytes 196616 | tf_op jit(solution)/shard_map/ppermute | solution.py:228
  22.3 1.4 %collective-permute-start.9 = (bf16[2,128,128]{2,1,0:T(8,128)(2,1)S(1)}, bf16[2,128,128]{2,1,0:T(8,128)(2,1)S(1)}, u32[]{:S(2)}, u32[]{:S(2)}) collective-permute-start(bf16[2,128,128]{2,1,0:T(8,128)(2,1)S(1)} %collective-permute-done.5.refs_2_), channel_id=1, source_target_pairs={{0,1},{1,0},{2,3},{3,2},{4,5},{5,4},{6,7},{7,6},{8,9},{9,8},{10,11... | collective-permute-start | bytes 196616 | tf_op jit(solution)/shard_map/ppermute | solution.py:228
  22.8 1.3 %collective-permute-start.10 = (bf16[2,128,128]{2,1,0:T(8,128)(2,1)S(1)}, bf16[2,128,128]{2,1,0:T(8,128)(2,1)S(1)}, u32[]{:S(2)}, u32[]{:S(2)}) collective-permute-start(bf16[2,128,128]{2,1,0:T(8,128)(2,1)S(1)} %collective-permute-done.6.refs_3_), channel_id=1, source_target_pairs={{0,1},{1,0},{2,3},{3,2},{4,5},{5,4},{6,7},{7,6},{8,9},{9,8},{10,11... | collective-permute-start | bytes 196616 | tf_op jit(solution)/shard_map/ppermute | solution.py:228

commit v5 on v4

--- a/solution.py
+++ b/solution.py
@@ -9,6 +9,7 @@
 
 BLOCKS = 8
 QUAD = 4
+SLOTS = 6
 CHUNK = 256
 FIRST = (3, 2, 1)
 SECOND = (3, 1, 2)
@@ -93,13 +94,14 @@
     edge_rows(chunk, scalar(scalars, 3), scalar(scalars, 0), read, gain_ref, w_ref, wg_ref, out_ref)
 
 
-def contract(places, small, which, part, left_ref, right_ref, lanes, store):
+def contract(places, small, which, part, left_ref, right_ref, lanes, slot, store):
     rows, tokens, channels = left_ref.shape
     depth = min(tokens, 128)
     for at_piece, (p, d) in enumerate(places):
         base = (part ^ p) * rows + (which ^ d) * small
-
-        def over(k, first, at_piece=at_piece):
+        skip = (slot + at_piece) % SLOTS * (small * rows + 1) * 8
+
+        def over(k, first, at_piece=at_piece, skip=skip):
             at = pl.ds(k * depth, depth)
             rights = [
                 right_ref[at_piece * small + t, at, :].astype(jnp.float32).reshape(-1, 8, channels)
@@ -108,7 +110,7 @@
             for i in range(rows):
                 l = left_ref[i, at, :].reshape(-1, 8, channels)
                 for t in range(small):
-                    here = pl.ds((t * rows + i) * 8, 8)
+                    here = pl.ds(skip + (t * rows + i) * 8, 8)
                     total = jnp.sum(l * rights[t], axis=0)
                     lanes[here, :] = total if first else lanes[here, :] + total
 
@@ -116,9 +118,9 @@
         if tokens > depth:
             pl.loop(1, tokens // depth)(lambda k: over(k, False))
         for t in range(small):
-            total = lanes[pl.ds(t * rows * 8, rows, stride=8), :]
+            total = lanes[pl.ds(skip + t * rows * 8, rows, stride=8), :]
             for s in range(1, 8):
-                total = total + lanes[pl.ds(t * rows * 8 + s, rows, stride=8), :]
+                total = total + lanes[pl.ds(skip + t * rows * 8 + s, rows, stride=8), :]
             store(base + t, at_piece * small + t, total)
 
 
@@ -135,7 +137,7 @@
         def store(j, held_at, total, at_row=at_row):
             product[at_row + held_at] = total
 
-        contract(places, small, scalar(scalars, 4), scalar(scalars, 5), left_ref, right_ref, lanes, store)
+        contract(places, small, scalar(scalars, 4), scalar(scalars, 5), left_ref, right_ref, lanes, at_row // small, store)
         at_row += right_ref.shape[0]
     out_ref[...] = project(product[...].reshape(-1, product.shape[-1]), w_out_ref, gain_ref).reshape(out_ref.shape)
 
@@ -156,7 +158,7 @@
         def store(j, held_at, total, at_row=at_row):
             product[at_row + held_at] = total
 
-        contract(places, small, which, part, left_ref, right_ref, lanes, store)
+        contract(places, small, which, part, left_ref, right_ref, lanes, at_row // small, store)
         at_row += right_ref.shape[0]
     late = project(product[...].reshape(-1, channels), w_out_ref, gain_ref)
     for at_piece, place in enumerate(sum(order, [])):
@@ -259,7 +261,7 @@
         order = order + [[(p ^ bit, d) for p, d in places] for places in order]
         bit *= 2
 
-    lanes = pltpu.VMEM(((small * rows + 1) * 8, channels), f32)
+    lanes = pltpu.VMEM((SLOTS * (small * rows + 1) * 8, channels), f32)
     groups = GROUPS if len(held) == 8 else (range(len(held)),)
     early, early_order = [], []
     for group in groups[:-1]:

time: 25.5 us -> 25.5 us (level)
  no operation moved by 1% of the time
where the time goes in v5:
time: 25.5 us; the launch traced here: 25.3 us
  starting transfers between devices  11.4 us (45%)
  waiting for transfers between devices  7.79 us (31%)
  Pallas kernels  3.08 us (12%)
  local copies, waits for them, and re-layouts  1.65 us (6%)
  between operations  1.38 us (5%)
    ppermute x11, starting transfers between devices, swap(): return lax.ppermute(values, 'row', [(i, i ^ mask) for i in range(devices)])  11.4 us
    ppermute x11, waiting for transfers between devices, swap(): return lax.ppermute(values, 'row', [(i, i ^ mask) for i in range(devices)])  7.79 us
    pallas_call x4, Pallas kernels, local(): pl.pallas_call(body, out_shape=out_shape, in_specs=[VMEM] * (1 + len(oper...  2.99 us
    slice x1, local copies, waits for them, and re-layouts, on_device(): pair_rows[d * small:(d + 1) * small]  0.96 us
    unnamed x18, local copies, waits for them, and re-layouts  0.69 us
  transfers between devices with their start and end apart: 11, of which 6 were waited for; matrix products, arithmetic and copies ran while one was open for 0% of the time, Pallas kernels for 6%

profile of v5, /device:TPU:0, one launch (start us, length us, event | category | flops | bytes accessed | tf_op | source)
XLA Modules:
  0.0 25.3 jit_solution(5025429406610652017)
XLA Ops:
  0.0 0.0 copy-start
  0.0 0.0 copy-start.2
  0.0 0.0 copy-start.3
  0.0 1.0 %fusion = (bf16[2,128,128]{2,1,0:T(8,128)(2,1)S(1)}, bf16[2,128,128]{2,1,0:T(8,128)(2,1)S(1)}, bf16[2,128,128]{2,1,0:T(8,128)(2,1)S(1)}) fusion(bf16[8,128,128]{2,1,0:T(8,128)(2,1)} %x_ref.1), kind=kLoop, calls=%fused_computation.1 | loop fusion | bytes 393216 | tf_op jit(solution)/shard_map/slice | solution.py:232
  1.0 3.0 %collective-permute-start = (bf16[2,128,128]{2,1,0:T(8,128)(2,1)S(1)}, bf16[2,128,128]{2,1,0:T(8,128)(2,1)S(1)}, u32[]{:S(2)}, u32[]{:S(2)}) collective-permute-start(bf16[2,128,128]{2,1,0:T(8,128)(2,1)S(1)} %get-tuple-element.21), channel_id=1, source_target_pairs={{0,2},{1,3},{2,0},{3,1},{4,6},{5,7},{6,4},{7,5},{8,10},{9,11},{10,... | collective-permute-start | bytes 196616 | tf_op jit(solution)/shard_map/ppermute | solution.py:230
  4.0 1.6 %collective-permute-start.1 = (bf16[2,128,128]{2,1,0:T(8,128)(2,1)S(1)}, bf16[2,128,128]{2,1,0:T(8,128)(2,1)S(1)}, u32[]{:S(2)}, u32[]{:S(2)}) collective-permute-start(bf16[2,128,128]{2,1,0:T(8,128)(2,1)S(1)} %get-tuple-element.20), channel_id=1, source_target_pairs={{0,4},{1,5},{2,6},{3,7},{4,0},{5,1},{6,2},{7,3},{8,12},{9,13},{10,... | collective-permute-start | bytes 196616 | tf_op jit(solution)/shard_map/ppermute | solution.py:230
  5.6 0.0 collective-permute-start.2
  6.9 0.0 copy-start.7
  6.9 0.0 copy-start.8
  6.9 0.6 %copy-done.7 = f32[128]{0:T(128)S(1)} copy-done((f32[128]{0:T(128)S(1)}, f32[128]{0:T(128)}, u32[]{:S(2)}) %copy-start.7) | copy-done | bytes 536
  7.5 0.0 copy-done.8
  7.6 0.1 shard_map.109
  7.6 0.0 collective-permute-done.refs_1_
  7.6 1.1 %collective-permute-done.1.refs_2_ = bf16[2,128,128]{2,1,0:T(8,128)(2,1)S(1)} collective-permute-done((bf16[2,128,128]{2,1,0:T(8,128)(2,1)S(1)}, bf16[2,128,128]{2,1,0:T(8,128)(2,1)S(1)}, u32[]{:S(2)}, u32[]{:S(2)}) %collective-permute-start.1) | collective-permute-done | bytes 65568 | tf_op jit(solution)/shard_map/ppermute | solution.py:230
  8.8 1.9 %collective-permute-done.2.refs_3_ = bf16[2,128,128]{2,1,0:T(8,128)(2,1)S(1)} collective-permute-done((bf16[2,128,128]{2,1,0:T(8,128)(2,1)S(1)}, bf16[2,128,128]{2,1,0:T(8,128)(2,1)S(1)}, u32[]{:S(2)}, u32[]{:S(2)}) %collective-permute-start.2) | collective-permute-done | bytes 65568 | tf_op jit(solution)/shard_map/ppermute | solution.py:230
  10.7 0.0 copy-done
  10.7 0.0 copy-done.2
  10.8 0.0 copy-done.3
  10.8 0.0 copy-start.4
  10.8 0.0 copy-start.5
  10.8 0.0 copy-start.6
  10.8 0.4 %shard_map.110 = bf16[2,128,128]{2,1,0:T(8,128)(2,1)S(1)} custom-call(s32[1,128]{1,0:T(1,128)S(1)} %get-tuple-element.12.scalars, bf16[8,128,128]{2,1,0:T(8,128)(2,1)S(1)} %copy-done, bf16[2,128,128]{2,1,0:T(8,128)(2,1)S(1)} %collective-permute-done.refs_1_, bf16[2,128,128]{2,1,0:T(8,128)(2,1)S(1)} %collective-permute-done.1.refs_2_, ...), custom_call_target="tpu_custom_call" | custom-call | tf_op jit(solution)/shard_map/pallas_call | solution.py:200
  11.2 2.7 %collective-permute-start.3 = (bf16[2,128,128]{2,1,0:T(8,128)(2,1)S(1)}, bf16[2,128,128]{2,1,0:T(8,128)(2,1)S(1)}, u32[]{:S(2)}, u32[]{:S(2)}) collective-permute-start(bf16[2,128,128]{2,1,0:T(8,128)(2,1)S(1)} %shard_map.110), channel_id=1, source_target_pairs={{0,8},{1,9},{2,10},{3,11},{4,12},{5,13},{6,14},{7,15},{8,0},{9,1},... | collective-permute-start | bytes 196616 | tf_op jit(solution)/shard_map/ppermute | solution.py:230
  13.9 0.0 copy-done.4
  13.9 0.0 copy-done.5
  13.9 0.0 copy-done.6
  13.9 0.7 %shard_map.111 = (f32[8,128,128]{2,1,0:T(8,128)S(1)}, f32[8,16,128]{2,1,0:T(8,128)S(1)}) custom-call(s32[1,128]{1,0:T(1,128)S(1)} %get-tuple-element.12.scalars, bf16[8,128,128]{2,1,0:T(8,128)(2,1)S(1)} %copy-done, f32[1,128]{1,0:T(1,128)S(1)} %get-tuple-element.13.refs_4_.gain_ref, bf16[128,128]{1,0:T(8,128)(2,1)S(1)} %copy-done.4, ...), custom_call_target="tpu_custom_call" | custom-call | tf_op jit(solution)/shard_map/pallas_call | solution.py:200
  14.6 2.5 %collective-permute-done.3 = bf16[2,128,128]{2,1,0:T(8,128)(2,1)S(1)} collective-permute-done((bf16[2,128,128]{2,1,0:T(8,128)(2,1)S(1)}, bf16[2,128,128]{2,1,0:T(8,128)(2,1)S(1)}, u32[]{:S(2)}, u32[]{:S(2)}) %collective-permute-start.3) | collective-permute-done | bytes 65568 | tf_op jit(solution)/shard_map/ppermute | solution.py:230
  17.0 0.0 copy-start.1
  17.0 0.3 %collective-permute-start.4 = (bf16[2,128,128]{2,1,0:T(8,128)(2,1)S(1)}, bf16[2,128,128]{2,1,0:T(8,128)(2,1)S(1)}, u32[]{:S(2)}, u32[]{:S(2)}) collective-permute-start(bf16[2,128,128]{2,1,0:T(8,128)(2,1)S(1)} %broadcast_select_fusion.refs_0_), channel_id=1, source_target_pairs={{0,6},{1,7},{2,4},{3,5},{4,2},{5,3},{6,0},{7,1},{8,14},{9,15},{10,... | collective-permute-start | bytes 196616 | tf_op jit(solution)/shard_map/ppermute | solution.py:230
  17.3 1.2 %collective-permute-start.5 = (bf16[2,128,128]{2,1,0:T(8,128)(2,1)S(1)}, bf16[2,128,128]{2,1,0:T(8,128)(2,1)S(1)}, u32[]{:S(2)}, u32[]{:S(2)}) collective-permute-start(bf16[2,128,128]{2,1,0:T(8,128)(2,1)S(1)} %broadcast_select_fusion.refs_0_), channel_id=1, source_target_pairs={{0,2},{1,3},{2,0},{3,1},{4,6},{5,7},{6,4},{7,5},{8,10},{9,11},{10,... | collective-permute-start | bytes 196616 | tf_op jit(solution)/shard_map/ppermute | solution.py:230
  18.5 2.1 %collective-permute-start.6 = (bf16[2,128,128]{2,1,0:T(8,128)(2,1)S(1)}, bf16[2,128,128]{2,1,0:T(8,128)(2,1)S(1)}, u32[]{:S(2)}, u32[]{:S(2)}) collective-permute-start(bf16[2,128,128]{2,1,0:T(8,128)(2,1)S(1)} %broadcast_select_fusion.refs_0_), channel_id=1, source_target_pairs={{0,4},{1,5},{2,6},{3,7},{4,0},{5,1},{6,2},{7,3},{8,12},{9,13},{10,... | collective-permute-start | bytes 196616 | tf_op jit(solution)/shard_map/ppermute | solution.py:230
  20.6 0.0 collective-permute-start.7
  20.6 1.7 %collective-permute-done.4.refs_1_ = bf16[2,128,128]{2,1,0:T(8,128)(2,1)S(1)} collective-permute-done((bf16[2,128,128]{2,1,0:T(8,128)(2,1)S(1)}, bf16[2,128,128]{2,1,0:T(8,128)(2,1)S(1)}, u32[]{:S(2)}, u32[]{:S(2)}) %collective-permute-start.4) | collective-permute-done | bytes 65568 | tf_op jit(solution)/shard_map/ppermute | solution.py:230
  22.3 0.0 collective-permute-start.8
  22.3 0.0 collective-permute-done.5.refs_2_
  22.3 0.5 %collective-permute-start.9 = (bf16[2,128,128]{2,1,0:T(8,128)(2,1)S(1)}, bf16[2,128,128]{2,1,0:T(8,128)(2,1)S(1)}, u32[]{:S(2)}, u32[]{:S(2)}) collective-permute-start(bf16[2,128,128]{2,1,0:T(8,128)(2,1)S(1)} %collective-permute-done.5.refs_2_), channel_id=1, source_target_pairs={{0,1},{1,0},{2,3},{3,2},{4,5},{5,4},{6,7},{7,6},{8,9},{9,8},{10,11... | collective-permute-start | bytes 196616 | tf_op jit(solution)/shard_map/ppermute | solution.py:230
  22.8 0.0 collective-permute-done.6.refs_3_
  22.8 0.0 collective-permute-start.10
  22.9 0.0 collective-permute-done.7.refs_4_
  22.9 0.0 copy-done.1
  22.9 0.7 %shard_map.112.refs_0_ = f32[10,8,128]{2,1,0:T(8,128)S(1)} custom-call(s32[1,128]{1,0:T(1,128)S(1)} %get-tuple-element.12.scalars, f32[8,128,128]{2,1,0:T(8,128)S(1)} %get-tuple-element.15.left_ref, bf16[128,128]{1,0:T(8,128)(2,1)S(1)} %copy-done.1, f32[1,128]{1,0:T(1,128)S(1)} %get-tuple-element.17.gain_ref, ...), custom_call_target="tpu_custom_call" | custom-call | tf_op jit(solution)/shard_map/pallas_call | solution.py:200
  23.6 0.0 collective-permute-done.8.refs_1_
  23.6 0.1 collective-permute-done.9.refs_2_
  23.7 0.4 %collective-permute-done.10.refs_3_ = bf16[2,128,128]{2,1,0:T(8,128)(2,1)S(1)} collective-permute-done((bf16[2,128,128]{2,1,0:T(8,128)(2,1)S(1)}, bf16[2,128,128]{2,1,0:T(8,128)(2,1)S(1)}, u32[]{:S(2)}, u32[]{:S(2)}) %collective-permute-start.10) | collective-permute-done | bytes 65568 | tf_op jit(solution)/shard_map/ppermute | solution.py:230
  24.1 1.2 %shard_map.113 = bf16[8,16,128]{2,1,0:T(8,128)(2,1)} custom-call(s32[1,128]{1,0:T(1,128)S(1)} %get-tuple-element.12.scalars, f32[8,128,128]{2,1,0:T(8,128)S(1)} %get-tuple-element.15.left_ref, f32[8,16,128]{2,1,0:T(8,128)S(1)} %get-tuple-element.16.gate_ref, bf16[128,128]{1,0:T(8,128)(2,1)S(1)} %copy-done.1, f32[1,128]{1,0:T(1,128)S(1)} %get-tuple-element.17.gain_ref, ...), custom_call_target="tpu_custom_call" | custom-call | tf_op jit(solution)/shard_map/pallas_call | solution.py:200
  (1 shorter events, 0.0 us)
Async XLA Ops:
  0.0 10.7 %copy-start = (bf16[8,128,128]{2,1,0:T(8,128)(2,1)S(1)}, bf16[8,128,128]{2,1,0:T(8,128)(2,1)}, u32[]{:S(2)}) copy-start(bf16[8,128,128]{2,1,0:T(8,128)(2,1)} %x_ref.1) | copy-start | bytes 786436
  0.0 10.7 %copy-start.2 = (bf16[128,128]{1,0:T(8,128)(2,1)S(1)}, bf16[128,128]{1,0:T(8,128)(2,1)}, u32[]{:S(2)}) copy-start(bf16[128,128]{1,0:T(8,128)(2,1)} %refs_5_.1) | copy-start | bytes 98308
  0.0 10.7 %copy-start.3 = (bf16[128,128]{1,0:T(8,128)(2,1)S(1)}, bf16[128,128]{1,0:T(8,128)(2,1)}, u32[]{:S(2)}) copy-start(bf16[128,128]{1,0:T(8,128)(2,1)} %refs_6_.1) | copy-start | bytes 98308
  1.0 6.7 %collective-permute-start = (bf16[2,128,128]{2,1,0:T(8,128)(2,1)S(1)}, bf16[2,128,128]{2,1,0:T(8,128)(2,1)S(1)}, u32[]{:S(2)}, u32[]{:S(2)}) collective-permute-start(bf16[2,128,128]{2,1,0:T(8,128)(2,1)S(1)} %get-tuple-element.21), channel_id=1, source_target_pairs={{0,2},{1,3},{2,0},{3,1},{4,6},{5,7},{6,4},{7,5},{8,10},{9,11},{10,... | collective-permute-start | bytes 196616 | tf_op jit(solution)/shard_map/ppermute | solution.py:230
  4.0 4.8 %collective-permute-start.1 = (bf16[2,128,128]{2,1,0:T(8,128)(2,1)S(1)}, bf16[2,128,128]{2,1,0:T(8,128)(2,1)S(1)}, u32[]{:S(2)}, u32[]{:S(2)}) collective-permute-start(bf16[2,128,128]{2,1,0:T(8,128)(2,1)S(1)} %get-tuple-element.20), channel_id=1, source_target_pairs={{0,4},{1,5},{2,6},{3,7},{4,0},{5,1},{6,2},{7,3},{8,12},{9,13},{10,... | collective-permute-start | bytes 196616 | tf_op jit(solution)/shard_map/ppermute | solution.py:230
  5.6 5.2 %collective-permute-start.2 = (bf16[2,128,128]{2,1,0:T(8,128)(2,1)S(1)}, bf16[2,128,128]{2,1,0:T(8,128)(2,1)S(1)}, u32[]{:S(2)}, u32[]{:S(2)}) collective-permute-start(bf16[2,128,128]{2,1,0:T(8,128)(2,1)S(1)} %get-tuple-element.19), channel_id=1, source_target_pairs={{0,6},{1,7},{2,4},{3,5},{4,2},{5,3},{6,0},{7,1},{8,14},{9,15},{10,... | collective-permute-start | bytes 196616 | tf_op jit(solution)/shard_map/ppermute | solution.py:230
  6.9 0.7 %copy-start.7 = (f32[128]{0:T(128)S(1)}, f32[128]{0:T(128)}, u32[]{:S(2)}) copy-start(f32[128]{0:T(128)} %param.12) | copy-start | bytes 1540
  6.9 0.7 %copy-start.8 = (f32[128]{0:T(128)S(1)}, f32[128]{0:T(128)}, u32[]{:S(2)}) copy-start(f32[128]{0:T(128)} %param.19) | copy-start | bytes 1540
  10.8 3.1 %copy-start.4 = (bf16[128,128]{1,0:T(8,128)(2,1)S(1)}, bf16[128,128]{1,0:T(8,128)(2,1)}, u32[]{:S(2)}) copy-start(bf16[128,128]{1,0:T(8,128)(2,1)} %w_ref.1) | copy-start | bytes 98308
  10.8 3.1 %copy-start.5 = (bf16[128,128]{1,0:T(8,128)(2,1)S(1)}, bf16[128,128]{1,0:T(8,128)(2,1)}, u32[]{:S(2)}) copy-start(bf16[128,128]{1,0:T(8,128)(2,1)} %wg_ref.1) | copy-start | bytes 98308
  10.8 3.1 %copy-start.6 = (bf16[128,128]{1,0:T(8,128)(2,1)S(1)}, bf16[128,128]{1,0:T(8,128)(2,1)}, u32[]{:S(2)}) copy-start(bf16[128,128]{1,0:T(8,128)(2,1)} %wo_ref.1) | copy-start | bytes 98308
  11.2 5.8 %collective-permute-start.3 = (bf16[2,128,128]{2,1,0:T(8,128)(2,1)S(1)}, bf16[2,128,128]{2,1,0:T(8,128)(2,1)S(1)}, u32[]{:S(2)}, u32[]{:S(2)}) collective-permute-start(bf16[2,128,128]{2,1,0:T(8,128)(2,1)S(1)} %shard_map.110), channel_id=1, source_target_pairs={{0,8},{1,9},{2,10},{3,11},{4,12},{5,13},{6,14},{7,15},{8,0},{9,1},... | collective-permute-start | bytes 196616 | tf_op jit(solution)/shard_map/ppermute | solution.py:230
  17.0 5.9 %copy-start.1 = (bf16[128,128]{1,0:T(8,128)(2,1)S(1)}, bf16[128,128]{1,0:T(8,128)(2,1)}, u32[]{:S(2)}) copy-start(bf16[128,128]{1,0:T(8,128)(2,1)} %w_out_ref.3) | copy-start | bytes 98308
  17.0 5.2 %collective-permute-start.4 = (bf16[2,128,128]{2,1,0:T(8,128)(2,1)S(1)}, bf16[2,128,128]{2,1,0:T(8,128)(2,1)S(1)}, u32[]{:S(2)}, u32[]{:S(2)}) collective-permute-start(bf16[2,128,128]{2,1,0:T(8,128)(2,1)S(1)} %broadcast_select_fusion.refs_0_), channel_id=1, source_target_pairs={{0,6},{1,7},{2,4},{3,5},{4,2},{5,3},{6,0},{7,1},{8,14},{9,15},{10,... | collective-permute-start | bytes 196616 | tf_op jit(solution)/shard_map/ppermute | solution.py:230
  17.3 5.0 %collective-permute-start.5 = (bf16[2,128,128]{2,1,0:T(8,128)(2,1)S(1)}, bf16[2,128,128]{2,1,0:T(8,128)(2,1)S(1)}, u32[]{:S(2)}, u32[]{:S(2)}) collective-permute-start(bf16[2,128,128]{2,1,0:T(8,128)(2,1)S(1)} %broadcast_select_fusion.refs_0_), channel_id=1, source_target_pairs={{0,2},{1,3},{2,0},{3,1},{4,6},{5,7},{6,4},{7,5},{8,10},{9,11},{10,... | collective-permute-start | bytes 196616 | tf_op jit(solution)/shard_map/ppermute | solution.py:230
  18.5 4.3 %collective-permute-start.6 = (bf16[2,128,128]{2,1,0:T(8,128)(2,1)S(1)}, bf16[2,128,128]{2,1,0:T(8,128)(2,1)S(1)}, u32[]{:S(2)}, u32[]{:S(2)}) collective-permute-start(bf16[2,128,128]{2,1,0:T(8,128)(2,1)S(1)} %broadcast_select_fusion.refs_0_), channel_id=1, source_target_pairs={{0,4},{1,5},{2,6},{3,7},{4,0},{5,1},{6,2},{7,3},{8,12},{9,13},{10,... | collective-permute-start | bytes 196616 | tf_op jit(solution)/shard_map/ppermute | solution.py:230
  20.6 2.3 %collective-permute-start.7 = (bf16[2,128,128]{2,1,0:T(8,128)(2,1)S(1)}, bf16[2,128,128]{2,1,0:T(8,128)(2,1)S(1)}, u32[]{:S(2)}, u32[]{:S(2)}) collective-permute-start(bf16[2,128,128]{2,1,0:T(8,128)(2,1)S(1)} %broadcast_select_fusion.refs_0_), channel_id=1, source_target_pairs={{0,1},{1,0},{2,3},{3,2},{4,5},{5,4},{6,7},{7,6},{8,9},{9,8},{10,11... | collective-permute-start | bytes 196616 | tf_op jit(solution)/shard_map/ppermute | solution.py:230
  22.3 1.3 %collective-permute-start.8 = (bf16[2,128,128]{2,1,0:T(8,128)(2,1)S(1)}, bf16[2,128,128]{2,1,0:T(8,128)(2,1)S(1)}, u32[]{:S(2)}, u32[]{:S(2)}) collective-permute-start(bf16[2,128,128]{2,1,0:T(8,128)(2,1)S(1)} %collective-permute-done.4.refs_1_), channel_id=1, source_target_pairs={{0,1},{1,0},{2,3},{3,2},{4,5},{5,4},{6,7},{7,6},{8,9},{9,8},{10,11... | collective-permute-start | bytes 196616 | tf_op jit(solution)/shard_map/ppermute | solution.py:230
  22.3 1.4 %collective-permute-start.9 = (bf16[2,128,128]{2,1,0:T(8,128)(2,1)S(1)}, bf16[2,128,128]{2,1,0:T(8,128)(2,1)S(1)}, u32[]{:S(2)}, u32[]{:S(2)}) collective-permute-start(bf16[2,128,128]{2,1,0:T(8,128)(2,1)S(1)} %collective-permute-done.5.refs_2_), channel_id=1, source_target_pairs={{0,1},{1,0},{2,3},{3,2},{4,5},{5,4},{6,7},{7,6},{8,9},{9,8},{10,11... | collective-permute-start | bytes 196616 | tf_op jit(solution)/shard_map/ppermute | solution.py:230
  22.8 1.3 %collective-permute-start.10 = (bf16[2,128,128]{2,1,0:T(8,128)(2,1)S(1)}, bf16[2,128,128]{2,1,0:T(8,128)(2,1)S(1)}, u32[]{:S(2)}, u32[]{:S(2)}) collective-permute-start(bf16[2,128,128]{2,1,0:T(8,128)(2,1)S(1)} %collective-permute-done.6.refs_3_), channel_id=1, source_target_pairs={{0,1},{1,0},{2,3},{3,2},{4,5},{5,4},{6,7},{7,6},{8,9},{9,8},{10,11... | collective-permute-start | bytes 196616 | tf_op jit(solution)/shard_map/ppermute | solution.py:230
